TPU v7x, 32 devices: a whole 2x2x4 slice. The times are simulated.
32 devices in a mesh: dp: 16 (over z, x, core), shard: 2 (over y).
Axes of the slice: x: 2, y: 2, z: 4, core: 2. Of those that a mesh axis runs over, the one named last changes fastest.
Arguments:
- tokens: bfloat16 [64, 1024, 960], P('dp', 'shard'), may hold values from -6 to 6
- positions: int32 [64, 1024], P('dp', 'shard'), may hold values from 0 to 1023, as said below
- attn_gain: bfloat16 [960], P('shard'), may hold values from 0.25 to 1.75
- w_query: bfloat16 [960, 960], P('shard'), may hold values from -0.375 to 0.375
- w_key: bfloat16 [960, 320], P('shard'), may hold values from -0.1875 to 0.1875
- w_value: bfloat16 [960, 320], P('shard'), may hold values from -0.1875 to 0.1875
- w_out: bfloat16 [960, 960], P('shard'), may hold values from -0.5 to 0.5
- mlp_gain: bfloat16 [960], P('shard'), may hold values from 0.25 to 1.75
- w_gate: bfloat16 [960, 2560], P('shard'), may hold values from -0.1875 to 0.1875
- w_up: bfloat16 [960, 2560], P('shard'), may hold values from -0.1875 to 0.1875
- w_down: bfloat16 [2560, 960], P('shard'), may hold values from -0.125 to 0.125
- cotangent: bfloat16 [64, 1024, 960], P('dp', 'shard'), may hold values from -6 to 6
Outputs:
- output: bfloat16 [64, 1024, 960], P('dp', 'shard')
- input_grad: float32 [64, 1024, 960], P('dp', 'shard')
- grad_attn_gain: float32 [960], P('shard')
- grad_query: float32 [960, 960], P('shard')
- grad_key: float32 [960, 320], P('shard')
- grad_value: float32 [960, 320], P('shard')
- grad_out: float32 [960, 960], P('shard')
- grad_mlp_gain: float32 [960], P('shard')
- grad_gate: float32 [960, 2560], P('shard')
- grad_up: float32 [960, 2560], P('shard')
- grad_down: float32 [2560, 960], P('shard')
Inputs may be any that keep to these rules, and one draw needn't show every extreme that they name: `positions`: in each row the first entry is 0 and every later entry is 0 or one more than the entry before it. In each aligned run of 4 rows one row, drawn from the seed, is the single document 0, 1, ..., 1023.
All inputs are finite; a program needn't handle non-finite values.
Results may differ from a plain program's by a relative error of at most 0.024.
Values may be sent and summed in bfloat16 or wider, within the bound.
A program may use at most 320 MiB of HBM per device.

v0:
```python
import jax
import jax.numpy as jnp
from jax import lax
from jax.sharding import PartitionSpec as P

HQ = 15
KVH = 5
HD = 64


NORM_EPSILON = 1e-05
ROPE_BASE = 100000.0


def normalize(values, gain_row):
    return (
        values * lax.rsqrt(jnp.mean(values * values, -1, keepdims=True) + NORM_EPSILON) * gain_row
    )


def rotate(values, places, head_count, direction):
    shaped = values.reshape(values.shape[0], values.shape[1], head_count, -1)
    half_size = shaped.shape[-1] // 2
    frequency = ROPE_BASE ** (-jnp.arange(half_size, dtype=jnp.float32) * 2.0 / (2 * half_size))
    angles = places.astype(jnp.float32)[:, :, None] * frequency[None, None, :]
    cosine = jnp.cos(angles)[:, :, None, :]
    sine_part = direction * jnp.sin(angles)[:, :, None, :]
    first_half = shaped[..., :half_size]
    second_half = shaped[..., half_size:]
    turned = jnp.concatenate(
        [
            first_half * cosine - second_half * sine_part,
            second_half * cosine + first_half * sine_part,
        ],
        -1,
    )
    return turned.reshape(values.shape)


def project_rows(left_side, weight):
    return jnp.einsum("sqd,de->sqe", left_side, weight, preferred_element_type=jnp.float32)


def project_back(grad_rows, weight):
    return jnp.einsum("sqe,de->sqd", grad_rows, weight, preferred_element_type=jnp.float32)


def weight_grad(left_side, grad_rows):
    return jnp.einsum("sqd,sqe->de", left_side, grad_rows, preferred_element_type=jnp.float32)


def gated(gate_in, up_in):
    return jax.nn.silu(gate_in) * up_in


def body(
    tokens,
    positions,
    attn_gain,
    w_query,
    w_key,
    w_value,
    w_out,
    mlp_gain,
    w_gate,
    w_up,
    w_down,
    cotangent,
):
    seq_local = tokens.shape[0]
    rows_local = tokens.shape[1]
    group_width = HQ // KVH
    scale_factor = HD ** (-0.5)
    query_index = lax.axis_index("shard") * rows_local + jnp.arange(rows_local, dtype=jnp.int32)
    doc_start = query_index[None, :] - positions
    full_query, full_key, full_value, full_out, first_gain = (
        lax.all_gather(w_query, "shard", axis=0, tiled=True),
        lax.all_gather(w_key, "shard", axis=0, tiled=True),
        lax.all_gather(w_value, "shard", axis=0, tiled=True),
        lax.all_gather(w_out, "shard", axis=0, tiled=True),
        lax.all_gather(attn_gain, "shard", axis=0, tiled=True),
    )
    tokens_wide = tokens.astype(jnp.float32)
    normed_one = normalize(tokens_wide, first_gain.astype(jnp.float32)).astype(jnp.bfloat16)
    query_rot = rotate(project_rows(normed_one, full_query), positions, HQ, 1.0).astype(
        jnp.bfloat16
    )
    key_rot = rotate(project_rows(normed_one, full_key), positions, KVH, 1.0).astype(jnp.bfloat16)
    value_rows = project_rows(normed_one, full_value).astype(jnp.bfloat16)
    query_split = query_rot.reshape(seq_local, rows_local, KVH, group_width, HD)
    key_piece = lax.all_gather(key_rot, "shard", axis=1, tiled=True)
    value_piece = lax.all_gather(value_rows, "shard", axis=1, tiled=True)
    piece_rows = key_piece.shape[1]
    key_index = jnp.arange(piece_rows, dtype=jnp.int32)

    def per_sequence(seq_parts):
        run_max, run_total, run_acc, query_one, key_one, value_one, start_one = seq_parts
        scores = (
            jnp.einsum(
                "qhgd,khd->hgqk",
                query_one,
                key_one.reshape(piece_rows, KVH, HD),
                preferred_element_type=jnp.float32,
            )
            * scale_factor
        )
        allowed = (key_index[None, :] <= query_index[:, None]) & (
            key_index[None, :] >= start_one[:, None]
        )
        masked = jnp.where(allowed, scores, -1e30)
        new_max = jnp.maximum(run_max, jnp.max(masked, -1))
        weights = jnp.where(allowed, jnp.exp(masked - new_max[..., None]), 0.0)
        factor = jnp.exp(run_max - new_max)
        new_total = run_total * factor + jnp.sum(weights, -1)
        update = jnp.einsum(
            "hgqk,khd->qhgd",
            weights.astype(jnp.bfloat16),
            value_one.reshape(piece_rows, KVH, HD),
            preferred_element_type=jnp.float32,
        )
        scaled = (
            run_acc.reshape(rows_local, KVH, group_width, HD)
            * jnp.transpose(factor, (2, 0, 1))[..., None]
        )
        return (new_max, new_total, (scaled + update).reshape(rows_local, HQ * HD))

    run_max = jnp.full((seq_local, KVH, group_width, rows_local), -1e30, jnp.float32)
    run_total = jnp.zeros((seq_local, KVH, group_width, rows_local), jnp.float32)
    run_acc = jnp.zeros((seq_local, rows_local, HQ * HD), jnp.float32)
    run_max, run_total, run_acc = lax.map(
        per_sequence, (run_max, run_total, run_acc, query_split, key_piece, value_piece, doc_start)
    )
    log_total = run_max + jnp.log(run_total)
    inverse = jnp.transpose(1.0 / run_total, (0, 3, 1, 2))[..., None]
    heads_out = (
        (run_acc.reshape(seq_local, rows_local, KVH, group_width, HD) * inverse)
        .reshape(seq_local, rows_local, HQ * HD)
        .astype(jnp.bfloat16)
    )
    mixed_rows = tokens_wide + project_rows(heads_out, full_out)
    full_gate, full_up, full_down, second_gain = (
        lax.all_gather(w_gate, "shard", axis=0, tiled=True),
        lax.all_gather(w_up, "shard", axis=0, tiled=True),
        lax.all_gather(w_down, "shard", axis=0, tiled=True),
        lax.all_gather(mlp_gain, "shard", axis=0, tiled=True),
    )
    normed_two = normalize(mixed_rows, second_gain.astype(jnp.float32)).astype(jnp.bfloat16)
    gate_rows = project_rows(normed_two, full_gate)
    up_rows = project_rows(normed_two, full_up)
    hidden = gated(gate_rows, up_rows).astype(jnp.bfloat16)
    output = (mixed_rows + project_rows(hidden, full_down)).astype(jnp.bfloat16)
    full_gate, full_up, full_down, second_gain = (
        lax.all_gather(w_gate, "shard", axis=0, tiled=True),
        lax.all_gather(w_up, "shard", axis=0, tiled=True),
        lax.all_gather(w_down, "shard", axis=0, tiled=True),
        lax.all_gather(mlp_gain, "shard", axis=0, tiled=True),
    )
    hidden_grad = project_back(cotangent, full_down)
    gated_again, gated_pull = jax.vjp(gated, gate_rows, up_rows)
    gate_wide, up_wide = gated_pull(hidden_grad)
    gate_grad = gate_wide.astype(jnp.bfloat16)
    up_grad = up_wide.astype(jnp.bfloat16)
    normed_two_grad = project_back(gate_grad, full_gate) + project_back(up_grad, full_up)
    norm_again, norm_pull = jax.vjp(normalize, mixed_rows, second_gain.astype(jnp.float32))
    mixed_part, second_gain_grad = norm_pull(normed_two_grad)
    mixed_grad = cotangent.astype(jnp.float32) + mixed_part
    down_grad = weight_grad(hidden, cotangent)
    gate_weight_grad = weight_grad(normed_two, gate_grad)
    up_weight_grad = weight_grad(normed_two, up_grad)
    mlp_owned = (
        lax.psum_scatter(
            gate_weight_grad.astype(jnp.bfloat16), "shard", scatter_dimension=0, tiled=True
        ).astype(jnp.float32),
        lax.psum_scatter(
            up_weight_grad.astype(jnp.bfloat16), "shard", scatter_dimension=0, tiled=True
        ).astype(jnp.float32),
        lax.psum_scatter(
            down_grad.astype(jnp.bfloat16), "shard", scatter_dimension=0, tiled=True
        ).astype(jnp.float32),
        lax.psum_scatter(
            second_gain_grad.astype(jnp.bfloat16), "shard", scatter_dimension=0, tiled=True
        ).astype(jnp.float32),
    )
    full_query, full_key, full_value, full_out, first_gain = (
        lax.all_gather(w_query, "shard", axis=0, tiled=True),
        lax.all_gather(w_key, "shard", axis=0, tiled=True),
        lax.all_gather(w_value, "shard", axis=0, tiled=True),
        lax.all_gather(w_out, "shard", axis=0, tiled=True),
        lax.all_gather(attn_gain, "shard", axis=0, tiled=True),
    )
    branch_grad = mixed_grad.astype(jnp.bfloat16)
    out_weight_grad = weight_grad(heads_out, branch_grad)
    heads_grad = project_back(branch_grad, full_out).astype(jnp.bfloat16)
    heads_split = heads_grad.reshape(seq_local, rows_local, KVH, group_width, HD)
    key_all, value_all = (
        lax.all_gather(key_rot, "shard", axis=1, tiled=True),
        lax.all_gather(value_rows, "shard", axis=1, tiled=True),
    )
    length_all = key_all.shape[1]
    key_index_all = jnp.arange(length_all, dtype=jnp.int32)

    def grad_sequence(seq_parts):
        query_one, key_one, value_one, grad_one, log_one, start_one = seq_parts
        keys_split = key_one.reshape(length_all, KVH, HD)
        values_split = value_one.reshape(length_all, KVH, HD)
        scores = (
            jnp.einsum("qhgd,khd->hgqk", query_one, keys_split, preferred_element_type=jnp.float32)
            * scale_factor
        )
        allowed = (key_index_all[None, :] <= query_index[:, None]) & (
            key_index_all[None, :] >= start_one[:, None]
        )
        masked = jnp.where(allowed, scores, -1e30)
        prob_rows = jnp.where(allowed, jnp.exp(masked - log_one[..., None]), 0.0)
        prob_grad = jnp.einsum(
            "qhgd,khd->hgqk", grad_one, values_split, preferred_element_type=jnp.float32
        )
        delta_rows = jnp.sum(prob_rows * prob_grad, -1, keepdims=True)
        score_grad = (prob_rows * (prob_grad - delta_rows)).astype(jnp.bfloat16)
        query_grad = (
            jnp.einsum("hgqk,khd->qhgd", score_grad, keys_split, preferred_element_type=jnp.float32)
            * scale_factor
        )
        key_grad = (
            jnp.einsum("hgqk,qhgd->khd", score_grad, query_one, preferred_element_type=jnp.float32)
            * scale_factor
        )
        value_grad = jnp.einsum(
            "hgqk,qhgd->khd",
            prob_rows.astype(jnp.bfloat16),
            grad_one,
            preferred_element_type=jnp.float32,
        )
        return (
            query_grad.reshape(rows_local, HQ * HD),
            key_grad.reshape(length_all, KVH * HD),
            value_grad.reshape(length_all, KVH * HD),
        )

    query_grads, key_grads, value_grads = lax.map(
        grad_sequence, (query_split, key_all, value_all, heads_split, log_total, doc_start)
    )
    key_share, value_share = (
        lax.psum_scatter(
            key_grads.astype(jnp.bfloat16), "shard", scatter_dimension=1, tiled=True
        ).astype(jnp.float32),
        lax.psum_scatter(
            value_grads.astype(jnp.bfloat16), "shard", scatter_dimension=1, tiled=True
        ).astype(jnp.float32),
    )
    query_back = rotate(query_grads, positions, HQ, -1.0).astype(jnp.bfloat16)
    key_back = rotate(key_share, positions, KVH, -1.0).astype(jnp.bfloat16)
    value_back = value_share.astype(jnp.bfloat16)
    query_weight_grad = weight_grad(normed_one, query_back)
    key_weight_grad = weight_grad(normed_one, key_back)
    value_weight_grad = weight_grad(normed_one, value_back)
    normed_one_grad = (
        project_back(query_back, full_query)
        + project_back(key_back, full_key)
        + project_back(value_back, full_value)
    )
    first_again, first_pull = jax.vjp(normalize, tokens_wide, first_gain.astype(jnp.float32))
    token_part, first_gain_grad = first_pull(normed_one_grad)
    input_grad = mixed_grad + token_part
    attn_owned = (
        lax.psum_scatter(
            query_weight_grad.astype(jnp.bfloat16), "shard", scatter_dimension=0, tiled=True
        ).astype(jnp.float32),
        lax.psum_scatter(
            key_weight_grad.astype(jnp.bfloat16), "shard", scatter_dimension=0, tiled=True
        ).astype(jnp.float32),
        lax.psum_scatter(
            value_weight_grad.astype(jnp.bfloat16), "shard", scatter_dimension=0, tiled=True
        ).astype(jnp.float32),
        lax.psum_scatter(
            out_weight_grad.astype(jnp.bfloat16), "shard", scatter_dimension=0, tiled=True
        ).astype(jnp.float32),
        lax.psum_scatter(
            first_gain_grad.astype(jnp.bfloat16), "shard", scatter_dimension=0, tiled=True
        ).astype(jnp.float32),
    )
    summed = (
        lax.psum(attn_owned[0].astype(jnp.bfloat16), "dp").astype(jnp.float32),
        lax.psum(attn_owned[1].astype(jnp.bfloat16), "dp").astype(jnp.float32),
        lax.psum(attn_owned[2].astype(jnp.bfloat16), "dp").astype(jnp.float32),
        lax.psum(attn_owned[3].astype(jnp.bfloat16), "dp").astype(jnp.float32),
        lax.psum(attn_owned[4].astype(jnp.bfloat16), "dp").astype(jnp.float32),
        lax.psum(mlp_owned[0].astype(jnp.bfloat16), "dp").astype(jnp.float32),
        lax.psum(mlp_owned[1].astype(jnp.bfloat16), "dp").astype(jnp.float32),
        lax.psum(mlp_owned[2].astype(jnp.bfloat16), "dp").astype(jnp.float32),
        lax.psum(mlp_owned[3].astype(jnp.bfloat16), "dp").astype(jnp.float32),
    )
    return (
        output,
        input_grad,
        summed[4],
        summed[0],
        summed[1],
        summed[2],
        summed[3],
        summed[8],
        summed[5],
        summed[6],
        summed[7],
    )


def solution(mesh):
    in_specs = (
        P("dp", "shard", None),
        P("dp", "shard"),
        P("shard"),
        P("shard", None),
        P("shard", None),
        P("shard", None),
        P("shard", None),
        P("shard"),
        P("shard", None),
        P("shard", None),
        P("shard", None),
        P("dp", "shard", None),
    )
    out_specs = (
        P("dp", "shard", None),
        P("dp", "shard", None),
        P("shard"),
        P("shard", None),
        P("shard", None),
        P("shard", None),
        P("shard", None),
        P("shard"),
        P("shard", None),
        P("shard", None),
        P("shard", None),
    )
    return jax.shard_map(body, mesh=mesh, in_specs=in_specs, out_specs=out_specs, check_vma=False)
```

profile of v0, /device:TPU:0, one launch (start us, length us, event | category | flops | bytes accessed | tf_op | source)
XLA Modules:
  0.0 1484.7 jit_solution(9672635570369899649)
XLA Ops:
  17.6 16.4 %all-gather.1 = bf16[2,480,320]{1,2,0:T(8,128)(2,1)S(1)} all-gather(bf16[1,480,320]{1,2,0:T(8,128)(2,1)} %bitcast.306), channel_id=1, replica_groups=mesh['dp'=16,'shard'=2] {'shard'}, dimensions={0}, use_global_device_ids=true | all-gather | bytes 921600 | tf_op jit(solution)/shard_map/all_gather | solution.py:79
  79.1 15.0 %all-gather.14.cloned.1.call-done = bf16[4,1024,320]{1,2,0:T(8,128)(2,1)} async-done(((bf16[4,512,320]{1,2,0:T(8,128)(2,1)}), bf16[4,1024,320]{1,2,0:T(8,128)(2,1)}) %all-gather.14.cloned.1.call-update) | async-done | bytes 2621456 | tf_op jit(solution)/shard_map/all_gather | solution.py:92
  94.2 41.2 %all-gather.10.cloned.1.call-done = bf16[4,1024,320]{1,2,0:T(8,128)(2,1)} async-done(((bf16[4,512,320]{1,2,0:T(8,128)(2,1)}), bf16[4,1024,320]{1,2,0:T(8,128)(2,1)}) %all-gather.10.cloned.1.call-update) | async-done | bytes 2621456 | tf_op jit(solution)/shard_map/all_gather | solution.py:91
  139.6 187.6 %while.32 = (s32[]{:T(128)}, f32[4,5,3,512]{3,2,1,0:T(4,128)S(1)}, f32[4,5,3,512]{3,2,1,0:T(4,128)S(1)}, f32[4,512,960]{1,2,0:T(8,128)}, s32[4,512]{1,0:T(4,128)...) while((s32[]{:T(128)}, f32[4,5,3,512]{3,2,1,0:T(4,128)S(1)}, ...), condition=%wide.region_4.5_spmd.clone.clone, body=%wide.region_1.4_spmd.clone.clone.sunk | while | flops 2117605376 | bytes 107702392 | solution.py:130
  169.9 15.5 %bitcast_add_fusion.3 = f32[512,5,3,64]{0,3,2,1:T(8,128)S(1)} fusion(bf16[1024,5,64,1]{0,2,3,1:T(8,128)(2,1)S(1)} %bitcast.297, f32[5,1024,512,3]{2,1,3,0:T(8,128)} %get-tuple-element.458, f32[5,3,512]{2,1,0:T(4,128)S(1)} %get-tuple-element.460, pred[512,1024]{0,1:T(8,128)(4,1)S(1)} %fusion.158, f32[512,5,3]{0,2,1:T(4,128)S(1)} %get-tuple-element.464), kind=kOutput, calls=%fused_computation.14.clone.1 | convolution fusion | flops 1046446080 | bytes 34664448 | tf_op jit(solution)/shard_map/while/body/eval_jaxpr/hgqk,khd->qhgd/dot_general | solution.py:115
  234.1 16.1 %fusion.159 = (f32[5,3,512]{2,1,0:T(4,128)S(1)}, f32[5,1024,512,3]{2,1,3,0:T(8,128)}) fusion(pred[512,1024]{0,1:T(8,128)(4,1)S(1)} %fusion.158, bf16[1024,5,64,1]{0,2,3,1:T(8,128)(2,1)S(1)} %bitcast.286, bf16[4,512,5,3,64]{1,4,3,2,0:T(8,128)(2,1)} %get-tuple-element.506, s32[]{:T(128)S(6)} %copy.71), kind=kOutput, calls=%fused_computation.6.clone.1 | convolution fusion | flops 1030218240 | bytes 33650692 | tf_op jit(solution)/shard_map/while/body/eval_jaxpr/qhgd,khd->hgqk/dot_general | solution.py:99
  309.8 15.4 %bitcast_add_fusion.3 = f32[512,5,3,64]{0,3,2,1:T(8,128)S(1)} fusion(bf16[1024,5,64,1]{0,2,3,1:T(8,128)(2,1)S(1)} %bitcast.297, f32[5,1024,512,3]{2,1,3,0:T(8,128)} %get-tuple-element.458, f32[5,3,512]{2,1,0:T(4,128)S(1)} %get-tuple-element.460, pred[512,1024]{0,1:T(8,128)(4,1)S(1)} %fusion.158, f32[512,5,3]{0,2,1:T(4,128)S(1)} %get-tuple-element.464), kind=kOutput, calls=%fused_computation.14.clone.1 | convolution fusion | flops 1046446080 | bytes 34664448 | tf_op jit(solution)/shard_map/while/body/eval_jaxpr/hgqk,khd->qhgd/dot_general | solution.py:115
  350.0 18.4 %fusion.69 = f32[4,512,2560]{2,1,0:T(8,128)} fusion(bf16[4,512,960]{1,2,0:T(8,128)(2,1)} %multiply_convert_fusion.2, bf16[960,2560]{1,0:T(8,128)(2,1)} %all-gather.20.cloned.1.call-done), kind=kOutput, calls=%fused_computation.113 | convolution fusion | flops 10066329600 | bytes 29818880 | tf_op jit(solution)/shard_map/sqd,de->sqe/dot_general | solution.py:41
  368.4 18.2 %fusion.63 = f32[4,512,2560]{2,1,0:T(8,128)} fusion(bf16[4,512,960]{1,2,0:T(8,128)(2,1)} %param.27, bf16[2560,960]{0,1:T(8,128)(2,1)} %all-gather.22.cloned.1.call-done), kind=kOutput, calls=%fused_computation.107 | convolution fusion | flops 10066329600 | bytes 29818880 | tf_op jit(solution)/shard_map/sqe,de->sqd/dot_general | solution.py:45
  386.5 36.1 %fusion.52 = (bf16[4,512,2560]{2,1,0:T(8,128)(2,1)}, bf16[4,512,2560]{2,1,0:T(8,128)(2,1)}, bf16[4,512,2560]{2,1,0:T(8,128)(2,1)}) fusion(f32[4,512,2560]{2,1,0:T(8,128)} %fusion.63, f32[4,512,2560]{2,1,0:T(8,128)} %fusion.69, bf16[4,512,960]{1,2,0:T(8,128)(2,1)} %multiply_convert_fusion.2, bf16[960,2560]{1,0:T(8,128)(2,1)} %all-gather.18.cloned.1.call-done), kind=kOutput, calls=%fused_computation.76 | convolution fusion | flops 10150215680 | bytes 82247680 | tf_op jit(solution)/shard_map/sqd,de->sqe/dot_general | solution.py:41
  422.7 16.5 %fusion.67 = f32[4,512,960]{1,2,0:T(8,128)} fusion(bf16[4,512,2560]{2,1,0:T(8,128)(2,1)} %get-tuple-element.311, bf16[960,2560]{1,0:T(8,128)(2,1)} %all-gather.20.cloned.1.call-done), kind=kOutput, calls=%fused_computation.111 | convolution fusion | flops 10066329600 | bytes 23265280 | tf_op jit(solution)/shard_map/sqe,de->sqd/dot_general | solution.py:45
  439.2 20.1 %multiply_reduce_fusion = (bf16[960]{0:T(1024)(128)(2,1)}, f32[4,512]{1,0:T(4,128)S(1)}, f32[4,512,960]{1,2,0:T(8,128)}) fusion(f32[4,512,960]{1,2,0:T(8,128)} %copy-done.4, f32[4,512]{1,0:T(4,128)S(1)} %fusion.91, f32[960]{0:T(1024)S(1)} %copy-done.27, f32[4,512,960]{1,2,0:T(8,128)} %fusion.67, bf16[4,512,2560]{2,1,0:T(8,128)(2,1)} %get-tuple-element.310, ...), kind=kOutput, calls=%fused_computation.101 | convolution fusion | flops 10080089088 | bytes 39016064 | tf_op jit(solution)/shard_map/sqe,de->sqd/dot_general | solution.py:45
  474.2 408.2 %while.33 = (s32[]{:T(128)}, f32[4,512,960]{1,2,0:T(8,128)}, bf16[4,1024,320]{1,2,0:T(8,128)(2,1)}, bf16[4,1024,320]{1,2,0:T(8,128)(2,1)}, bf16[4,1024,320]{1,2,...) while((s32[]{:T(128)}, f32[4,512,960]{1,2,0:T(8,128)}, ...), condition=%wide.region_9.10_spmd.clone.clone, body=%wide.region_7.9_spmd.clone.clone.sunk | while | flops 5114520576 | bytes 255492256 | solution.py:240
  492.3 23.6 %fusion.173 = (f32[5,3,512]{2,1,0:T(4,128)S(1)}, f32[5,3,512,1024]{2,3,1,0:T(8,128)}) fusion(f32[5,1024,512,3]{2,1,3,0:T(8,128)} %fusion.171, f32[5,3,512]{2,1,0:T(4,128)S(1)} %dynamic-slice_bitcast_fusion.2, bf16[1024,5,64,1]{0,2,3,1:T(8,128)(2,1)S(1)} %bitcast.287, bf16[4,512,5,3,64]{1,4,3,2,0:T(8,128)(2,1)} %get-tuple-element.540, s32[]{:T(128)S(6)} %copy.83, ...), kind=kOutput, calls=%fused_computation.37.clone.1 | convolution fusion | flops 1053811200 | bytes 65138692 | tf_op jit(solution)/shard_map/while/body/eval_jaxpr/qhgd,khd->hgqk/dot_general | solution.py:207
  515.9 26.3 %fusion.174 = bf16[5,3,512,1024]{2,3,1,0:T(8,128)(2,1)} fusion(f32[5,3,512,1024]{2,3,1,0:T(8,128)} %get-tuple-element.476, f32[5,1024,512,3]{2,1,3,0:T(8,128)} %fusion.171, f32[5,3,512]{2,1,0:T(4,128)S(1)} %get-tuple-element.477), kind=kLoop, calls=%fused_computation.39.clone.1 | loop fusion | flops 23592960 | bytes 78673920 | tf_op jit(solution)/shard_map/while/body/eval_jaxpr/convert_element_type | solution.py:219
  594.3 23.6 %fusion.173 = (f32[5,3,512]{2,1,0:T(4,128)S(1)}, f32[5,3,512,1024]{2,3,1,0:T(8,128)}) fusion(f32[5,1024,512,3]{2,1,3,0:T(8,128)} %fusion.171, f32[5,3,512]{2,1,0:T(4,128)S(1)} %dynamic-slice_bitcast_fusion.2, bf16[1024,5,64,1]{0,2,3,1:T(8,128)(2,1)S(1)} %bitcast.287, bf16[4,512,5,3,64]{1,4,3,2,0:T(8,128)(2,1)} %get-tuple-element.540, s32[]{:T(128)S(6)} %copy.83, ...), kind=kOutput, calls=%fused_computation.37.clone.1 | convolution fusion | flops 1053811200 | bytes 65138692 | tf_op jit(solution)/shard_map/while/body/eval_jaxpr/qhgd,khd->hgqk/dot_general | solution.py:207
  617.9 26.3 %fusion.174 = bf16[5,3,512,1024]{2,3,1,0:T(8,128)(2,1)} fusion(f32[5,3,512,1024]{2,3,1,0:T(8,128)} %get-tuple-element.476, f32[5,1024,512,3]{2,1,3,0:T(8,128)} %fusion.171, f32[5,3,512]{2,1,0:T(4,128)S(1)} %get-tuple-element.477), kind=kLoop, calls=%fused_computation.39.clone.1 | loop fusion | flops 23592960 | bytes 78673920 | tf_op jit(solution)/shard_map/while/body/eval_jaxpr/convert_element_type | solution.py:219
  696.3 23.6 %fusion.173 = (f32[5,3,512]{2,1,0:T(4,128)S(1)}, f32[5,3,512,1024]{2,3,1,0:T(8,128)}) fusion(f32[5,1024,512,3]{2,1,3,0:T(8,128)} %fusion.171, f32[5,3,512]{2,1,0:T(4,128)S(1)} %dynamic-slice_bitcast_fusion.2, bf16[1024,5,64,1]{0,2,3,1:T(8,128)(2,1)S(1)} %bitcast.287, bf16[4,512,5,3,64]{1,4,3,2,0:T(8,128)(2,1)} %get-tuple-element.540, s32[]{:T(128)S(6)} %copy.83, ...), kind=kOutput, calls=%fused_computation.37.clone.1 | convolution fusion | flops 1053811200 | bytes 65138692 | tf_op jit(solution)/shard_map/while/body/eval_jaxpr/qhgd,khd->hgqk/dot_general | solution.py:207
  719.9 26.3 %fusion.174 = bf16[5,3,512,1024]{2,3,1,0:T(8,128)(2,1)} fusion(f32[5,3,512,1024]{2,3,1,0:T(8,128)} %get-tuple-element.476, f32[5,1024,512,3]{2,1,3,0:T(8,128)} %fusion.171, f32[5,3,512]{2,1,0:T(4,128)S(1)} %get-tuple-element.477), kind=kLoop, calls=%fused_computation.39.clone.1 | loop fusion | flops 23592960 | bytes 78673920 | tf_op jit(solution)/shard_map/while/body/eval_jaxpr/convert_element_type | solution.py:219
  798.3 23.6 %fusion.173 = (f32[5,3,512]{2,1,0:T(4,128)S(1)}, f32[5,3,512,1024]{2,3,1,0:T(8,128)}) fusion(f32[5,1024,512,3]{2,1,3,0:T(8,128)} %fusion.171, f32[5,3,512]{2,1,0:T(4,128)S(1)} %dynamic-slice_bitcast_fusion.2, bf16[1024,5,64,1]{0,2,3,1:T(8,128)(2,1)S(1)} %bitcast.287, bf16[4,512,5,3,64]{1,4,3,2,0:T(8,128)(2,1)} %get-tuple-element.540, s32[]{:T(128)S(6)} %copy.83, ...), kind=kOutput, calls=%fused_computation.37.clone.1 | convolution fusion | flops 1053811200 | bytes 65138692 | tf_op jit(solution)/shard_map/while/body/eval_jaxpr/qhgd,khd->hgqk/dot_general | solution.py:207
  821.9 26.3 %fusion.174 = bf16[5,3,512,1024]{2,3,1,0:T(8,128)(2,1)} fusion(f32[5,3,512,1024]{2,3,1,0:T(8,128)} %get-tuple-element.476, f32[5,1024,512,3]{2,1,3,0:T(8,128)} %fusion.171, f32[5,3,512]{2,1,0:T(4,128)S(1)} %get-tuple-element.477), kind=kLoop, calls=%fused_computation.39.clone.1 | loop fusion | flops 23592960 | bytes 78673920 | tf_op jit(solution)/shard_map/while/body/eval_jaxpr/convert_element_type | solution.py:219
  883.5 36.9 %reduce-scatter.16.cloned.1.call-done = bf16[4,512,320]{1,2,0:T(8,128)(2,1)} async-done(((bf16[4,1024,320]{1,2,0:T(8,128)(2,1)}), bf16[4,512,320]{1,2,0:T(8,128)(2,1)}) %reduce-scatter.16.cloned.1.call-update) | async-done | bytes 1310736 | tf_op jit(solution)/shard_map/reduce_scatter | solution.py:247
  925.8 35.2 %reduce-scatter.14.cloned.1.call-done = bf16[4,512,320]{1,2,0:T(8,128)(2,1)} async-done(((bf16[4,1024,320]{1,2,0:T(8,128)(2,1)}), bf16[4,512,320]{1,2,0:T(8,128)(2,1)}) %reduce-scatter.14.cloned.1.call-update) | async-done | bytes 1310736 | tf_op jit(solution)/shard_map/reduce_scatter | solution.py:244
  990.9 15.7 %bitcast_convert_fusion = bf16[2560,960]{0,1:T(8,128)(2,1)} fusion(bf16[4,512,960]{1,2,0:T(8,128)(2,1)} %param.27, bf16[4,512,2560]{2,1,0:T(8,128)(2,1)} %get-tuple-element.312), kind=kOutput, calls=%fused_computation.88 | convolution fusion | flops 10068787200 | bytes 19333120 | tf_op jit(solution)/shard_map/sqd,sqe->de/dot_general | solution.py:49
  1006.7 16.3 %bitcast_convert_fusion.2 = bf16[960,2560]{1,0:T(8,128)(2,1)} fusion(bf16[4,512,960]{1,2,0:T(8,128)(2,1)} %multiply_convert_fusion.2, bf16[4,512,2560]{2,1,0:T(8,128)(2,1)} %get-tuple-element.310), kind=kOutput, calls=%fused_computation.90 | convolution fusion | flops 10068787200 | bytes 19333120 | tf_op jit(solution)/shard_map/sqd,sqe->de/dot_general | solution.py:49
  1023.0 15.6 %bitcast_convert_fusion.1 = bf16[960,2560]{1,0:T(8,128)(2,1)} fusion(bf16[4,512,960]{1,2,0:T(8,128)(2,1)} %multiply_convert_fusion.2, bf16[4,512,2560]{2,1,0:T(8,128)(2,1)} %get-tuple-element.311), kind=kOutput, calls=%fused_computation.89 | convolution fusion | flops 10068787200 | bytes 19333120 | tf_op jit(solution)/shard_map/sqd,sqe->de/dot_general | solution.py:49
  1065.6 64.9 %reduce-scatter.26.cloned.1.call-done = bf16[1280,960]{0,1:T(8,128)(2,1)} async-done(((bf16[2560,960]{0,1:T(8,128)(2,1)}), bf16[1280,960]{0,1:T(8,128)(2,1)}) %reduce-scatter.26.cloned.1.call-update) | async-done | bytes 2457616 | tf_op jit(solution)/shard_map/reduce_scatter | solution.py:177
  1130.6 64.9 %reduce-scatter.22.cloned.1.call-done = bf16[480,2560]{1,0:T(8,128)(2,1)} async-done(((bf16[960,2560]{1,0:T(8,128)(2,1)}), bf16[480,2560]{1,0:T(8,128)(2,1)}) %reduce-scatter.22.cloned.1.call-update) | async-done | bytes 2457616 | tf_op jit(solution)/shard_map/reduce_scatter | solution.py:171
  1195.4 64.9 %reduce-scatter.24.cloned.1.call-done = bf16[480,2560]{1,0:T(8,128)(2,1)} async-done(((bf16[960,2560]{1,0:T(8,128)(2,1)}), bf16[480,2560]{1,0:T(8,128)(2,1)}) %reduce-scatter.24.cloned.1.call-update) | async-done | bytes 2457616 | tf_op jit(solution)/shard_map/reduce_scatter | solution.py:174
  1260.4 17.0 %add_convert_fusion = bf16[4,512,960]{1,2,0:T(8,128)(2,1)} fusion(f32[4,512,960]{1,2,0:T(8,128)} %copy-done.4, bf16[4,512,2560]{2,1,0:T(8,128)(2,1)} %get-tuple-element.312, bf16[2560,960]{0,1:T(8,128)(2,1)} %all-gather.22.cloned.1.call-done), kind=kOutput, calls=%fused_computation.104 | convolution fusion | flops 10070261760 | bytes 27197440 | tf_op jit(solution)/shard_map/sqd,de->sqe/dot_general | solution.py:41
  1294.2 34.6 %all-reduce.4 = (bf16[480]{0:T(512)(128)(2,1)S(1)}, bf16[480]{0:T(512)(128)(2,1)S(1)}) all-reduce(bf16[480]{0:T(512)(128)(2,1)S(1)} %dynamic-slice.3, bf16[480]{0:T(512)(128)(2,1)S(1)} %dynamic-slice.5), channel_id=1, replica_groups=mesh['dp'=16,'shard'=2] {'dp'}, use_global_device_ids=true, to_apply=%region_15.16 | all-reduce | flops 960 | bytes 3840 | tf_op jit(solution)/shard_map/psum | solution.py:287
  1341.4 120.0 %all-reduce.10.cloned.1.call-done = (bf16[480,960]{1,0:T(8,128)(2,1)}, bf16[480,320]{0,1:T(8,128)(2,1)}, bf16[480,320]{0,1:T(8,128)(2,1)}, bf16[480,960]{1,0:T(8...) async-done(((bf16[480,960]{1,0:T(8,128)(2,1)}, bf16[480,320]{0,1:T(8,128)(2,1)}, bf16[480,320]{0,1:T(8,128)(2,1)}, ...) | async-done | bytes 9830416 | tf_op jit(solution)/shard_map/psum | solution.py:283
  (269 shorter events, 553.3 us)
Async XLA Ops:
  7.2 60.1 %all-gather.12.cloned.1.call-start = ((), (), s32[]{:S(2)}) async-start(), calls=%async_computation.10 | async-start | bytes 2949120 | tf_op jit(solution)/shard_map/all_gather | solution.py:77
  7.9 86.2 %all-gather.14.cloned.1.call-start = ((), (), s32[]{:S(2)}) async-start(), calls=%async_computation.11 | async-start | bytes 3932160 | tf_op jit(solution)/shard_map/all_gather | solution.py:92
  17.6 49.7 %copy-start.25 = (f32[960]{0:T(1024)}, f32[960]{0:T(1024)S(1)}, u32[]{:S(2)}) copy-start(f32[960]{0:T(1024)S(1)} %convert_element_type.158) | copy-start | bytes 11524
  38.4 28.9 %copy-start.21 = (f32[4,512]{1,0:T(4,128)}, f32[4,512]{1,0:T(4,128)S(1)}, u32[]{:S(2)}) copy-start(f32[4,512]{1,0:T(4,128)S(1)} %fusion.90) | copy-start | bytes 24580
  43.3 13.2 copy-start.30
  43.3 92.0 %all-gather.10.cloned.1.call-start = ((), (), s32[]{:S(2)}) async-start(), calls=%async_computation.9 | async-start | bytes 3932160 | tf_op jit(solution)/shard_map/all_gather | solution.py:91
  58.3 17.0 %copy-start.5 = (f32[4,512,32]{1,2,0:T(8,128)}, f32[4,512,32]{1,2,0:T(8,128)S(1)}, u32[]{:S(2)}) copy-start(f32[4,512,32]{1,2,0:T(8,128)S(1)} %get-tuple-element.325) | copy-start | bytes 786436
  63.9 270.4 %all-gather.16.cloned.1.call-start = ((), (), s32[]{:S(2)}) async-start(), calls=%async_computation.12 | async-start | bytes 2949120 | tf_op jit(solution)/shard_map/all_gather | solution.py:80
  64.5 285.5 %all-gather.20.cloned.1.call-start = ((), (), s32[]{:S(2)}) async-start(), calls=%async_computation.14 | async-start | bytes 7372800 | tf_op jit(solution)/shard_map/all_gather | solution.py:143
  65.1 303.3 %all-gather.22.cloned.1.call-start = ((), (), s32[]{:S(2)}) async-start(), calls=%async_computation.15 | async-start | bytes 7372800 | tf_op jit(solution)/shard_map/all_gather | solution.py:144
  65.6 320.9 %all-gather.18.cloned.1.call-start = ((), (), s32[]{:S(2)}) async-start(), calls=%async_computation.13 | async-start | bytes 7372800 | tf_op jit(solution)/shard_map/all_gather | solution.py:142
  66.4 854.0 %reduce-scatter.16.cloned.1.call-start = ((), (), s32[]{:S(2)}) async-start(), calls=%async_computation.17 | async-start | bytes 3932160 | tf_op jit(solution)/shard_map/reduce_scatter | solution.py:247
  334.3 13.0 copy-start.27
  439.2 20.1 %slice-start = ((s8[7864320]{0:T(1024)(128)(4,1)}), s8[4194304]{0:T(1024)(128)(4,1)S(1)}, s32[]{:S(2)}) async-start(s8[7864320]{0:T(1024)(128)(4,1)} %bitcast.293), calls=%async_computation.26 | async-start | bytes 8388608
  439.2 20.1 %copy-start.29 = (f32[4,512]{1,0:T(4,128)S(1)}, f32[4,512]{1,0:T(4,128)}, u32[]{:S(2)}) copy-start(f32[4,512]{1,0:T(4,128)} %copy-done.28) | copy-start | bytes 24580
  439.2 20.2 %slice-start.1 = ((s8[7864320]{0:T(1024)(128)(4,1)}), s8[3670016]{0:T(1024)(128)(4,1)S(1)}, s32[]{:S(2)}) async-start(s8[7864320]{0:T(1024)(128)(4,1)} %bitcast.293), calls=%async_computation.27 | async-start | bytes 7340032
  439.2 20.2 %copy-start.7 = (bf16[4,512,960]{1,2,0:T(8,128)(2,1)S(1)}, bf16[4,512,960]{1,2,0:T(8,128)(2,1)}, u32[]{:S(2)}) copy-start(bf16[4,512,960]{1,2,0:T(8,128)(2,1)} %param.27) | copy-start | bytes 11796484
  882.4 38.0 %copy-start.22 = (f32[4,512]{1,0:T(4,128)S(1)}, f32[4,512]{1,0:T(4,128)}, u32[]{:S(2)}) copy-start(f32[4,512]{1,0:T(4,128)} %copy-done.21) | copy-start | bytes 24580
  882.4 38.0 %copy-start.26 = (f32[960]{0:T(1024)S(1)}, f32[960]{0:T(1024)}, u32[]{:S(2)}) copy-start(f32[960]{0:T(1024)} %copy-done.25) | copy-start | bytes 11524
  882.5 78.5 %reduce-scatter.14.cloned.1.call-start = ((), (), s32[]{:S(2)}) async-start(), calls=%async_computation.16 | async-start | bytes 3932160 | tf_op jit(solution)/shard_map/reduce_scatter | solution.py:244
  883.2 167.1 %reduce-scatter.30.cloned.1.call-start = ((), (), s32[]{:S(2)}) async-start(), calls=%async_computation.24 | async-start | bytes 1105920
  924.5 38.2 %copy-start.6 = (f32[4,512,32]{1,2,0:T(8,128)S(1)}, f32[4,512,32]{1,2,0:T(8,128)}, u32[]{:S(2)}) copy-start(f32[4,512,32]{1,2,0:T(8,128)} %copy-done.5) | copy-start | bytes 786436
  924.6 38.2 %copy-start.16 = (f32[4,512,32]{1,2,0:T(8,128)S(1)}, f32[4,512,32]{1,2,0:T(8,128)}, u32[]{:S(2)}) copy-start(f32[4,512,32]{1,2,0:T(8,128)} %get-tuple-element.323) | copy-start | bytes 786436
  925.8 126.4 %reduce-scatter.28.cloned.1.call-start = ((), (), s32[]{:S(2)}) async-start(), calls=%async_computation.23 | async-start | bytes 1105920
  966.3 87.7 %reduce-scatter.20.cloned.1.call-start = ((), (), s32[]{:S(2)}) async-start(), calls=%async_computation.19 | async-start | bytes 2949120 | tf_op jit(solution)/shard_map/reduce_scatter | solution.py:275
  976.6 89.0 %reduce-scatter.18.cloned.1.call-start = ((), (), s32[]{:S(2)}) async-start(), calls=%async_computation.18 | async-start | bytes 2949120 | tf_op jit(solution)/shard_map/reduce_scatter | solution.py:266
  990.5 140.1 %reduce-scatter.26.cloned.1.call-start = ((), (), s32[]{:S(2)}) async-start(), calls=%async_computation.22 | async-start | bytes 7372800 | tf_op jit(solution)/shard_map/reduce_scatter | solution.py:177
  1006.6 188.8 %reduce-scatter.22.cloned.1.call-start = ((), (), s32[]{:S(2)}) async-start(), calls=%async_computation.20 | async-start | bytes 7372800 | tf_op jit(solution)/shard_map/reduce_scatter | solution.py:171
  1023.0 237.4 %reduce-scatter.24.cloned.1.call-start = ((), (), s32[]{:S(2)}) async-start(), calls=%async_computation.21 | async-start | bytes 7372800 | tf_op jit(solution)/shard_map/reduce_scatter | solution.py:174
  1038.7 422.8 %all-reduce.10.cloned.1.call-start = ((), (), s32[]{:S(2)}) async-start(), calls=%async_computation.25 | async-start | bytes 19988480 | tf_op jit(solution)/shard_map/psum | solution.py:283
  1260.4 17.0 %copy-start.10 = (bf16[960,320,1]{0,1,2:T(8,128)(2,1)S(1)}, bf16[960,320,1]{0,1,2:T(8,128)(2,1)}, u32[]{:S(2)}) copy-start(bf16[960,320,1]{0,1,2:T(8,128)(2,1)} %copy-done.9) | copy-start | bytes 1843204
  1280.2 49.8 %copy-start.24 = (f32[4,512]{1,0:T(4,128)S(1)}, f32[4,512]{1,0:T(4,128)}, u32[]{:S(2)}) copy-start(f32[4,512]{1,0:T(4,128)} %copy-done.23) | copy-start | bytes 24580
  (20 other events, 92.3 us)
Sparse Core Ops, SparseCore 0:
  9.6 42.1 all-gather.11
  53.9 40.1 all-gather.13
  96.3 39.0 all-gather.9
  136.7 31.6 all-gather.15
  169.8 64.8 all-gather.19
  236.1 64.8 all-gather.21
  302.6 64.8 all-gather.17
  882.6 37.7 reduce-scatter.15
  923.3 37.5 reduce-scatter.13
  963.1 16.8 reduce-scatter.29
  982.3 16.8 reduce-scatter.27
  1001.9 30.4 reduce-scatter.19
  1035.2 30.3 reduce-scatter.17
  1068.4 62.1 reduce-scatter.25
  1133.3 62.0 reduce-scatter.21
  1198.2 62.1 reduce-scatter.23
  1265.0 196.3 all-reduce.9
where the time goes:
time: 1490 us; the launch traced here: 1480 us
  matrix products  641 us (43%)
  waiting for transfers between devices  458 us (31%)
  other arithmetic  229 us (15%)
  blocking collectives  73.6 us (5%)
  local copies, waits for them, and re-layouts  63.7 us (4%)
  between operations  16 us (1%)
    psum x1, waiting for transfers between devices, body(): lax.psum(attn_owned[0].astype(jnp.bfloat16), 'dp').astype(jnp.float32)  120 us
    convert_element_type x4, other arithmetic, grad_sequence(): score_grad = (prob_rows * (prob_grad - delta_rows)).astype(jnp.bfloat16)  105 us
    dot_general x7, matrix products, project_rows(): jnp.einsum('sqd,de->sqe', left_side, weight, preferred_element_type=jnp.f...  98 us
    dot_general x4, matrix products, grad_sequence(): jnp.einsum('qhgd,khd->hgqk', query_one, keys_split, preferred_element_typ...  94.3 us
    dot_general x7, matrix products, project_back(): jnp.einsum('sqe,de->sqd', grad_rows, weight, preferred_element_type=jnp.f...  82.8 us
    dot_general x7, matrix products, weight_grad(): jnp.einsum('sqd,sqe->de', left_side, grad_rows, preferred_element_type=jn...  69 us
    reduce_scatter x1, waiting for transfers between devices, body(): lax.psum_scatter(down_grad.astype(jnp.bfloat16), 'shard', scatter_dimensi...  64.9 us
    reduce_scatter x1, waiting for transfers between devices, body(): lax.psum_scatter(up_weight_grad.astype(jnp.bfloat16), 'shard', scatter_di...  64.9 us
  transfers between devices with their start and end apart: 17, of which 9 were waited for; matrix products, arithmetic and copies ran while one was open for 28% of the time, Pallas kernels for 0%

commit v1 on v0

v1 whole, which is shorter than its diff:
```python
import functools

import jax
import jax.numpy as jnp
from jax import lax
from jax.experimental import pallas as pl
from jax.experimental.pallas import tpu as pltpu
from jax.sharding import PartitionSpec as P

HQ = 15
KVH = 5
HD = 64
GROUP = HQ // KVH
BLOCK = 256


NORM_EPSILON = 1e-05
ROPE_BASE = 100000.0


def normalize(values, gain_row):
    return (
        values * lax.rsqrt(jnp.mean(values * values, -1, keepdims=True) + NORM_EPSILON) * gain_row
    )


def turn(values, cosine, sine_part):
    half = HD // 2
    first_half = values[..., :half, :]
    second_half = values[..., half:, :]
    return jnp.concatenate(
        [
            first_half * cosine - second_half * sine_part,
            second_half * cosine + first_half * sine_part,
        ],
        -2,
    )


def rotate_heads(values, cosine, sine_part):
    shaped = values.reshape(values.shape[0], -1, HD, values.shape[2])
    return turn(shaped, cosine[:, None], sine_part[:, None]).reshape(values.shape)


def mm(a, b):
    return lax.dot_general(a, b, (((1,), (0,)), ((), ())), preferred_element_type=jnp.float32)


def tile_rows(rows):
    return min(BLOCK, rows)


def tile_bias(tile, query_first, start_row):
    size = start_row.shape[1]
    keys = tile * size + lax.broadcasted_iota(jnp.int32, (size, size), 0)
    queries = query_first + lax.broadcasted_iota(jnp.int32, (size, size), 1)
    return jnp.where((keys <= queries) & (keys >= start_row), 0.0, -1e30)


def attend_kernel(
    meta, query_ref, cos_ref, sin_ref, key_ref, value_ref, start_ref,
    out_ref, turned_ref, log_ref, keys_flat,
):
    seq = pl.program_id(0)
    pieces, rows = key_ref.shape[0], key_ref.shape[3]
    tile_size = tile_rows(rows)
    per_piece = rows // tile_size
    for piece in range(pieces):
        keys_flat[piece * rows : (piece + 1) * rows, :] = key_ref[piece, 0].T
    cosine, sine_part = cos_ref[0], sin_ref[0]
    for head in range(GROUP):
        raw = query_ref[0, head * HD : (head + 1) * HD, :]
        turned = turn(raw, cosine, sine_part).astype(jnp.bfloat16)
        turned_ref[0, head * HD : (head + 1) * HD, :] = turned * jnp.bfloat16(HD**-0.5)
    for block in range(per_piece):
        span = slice(block * tile_size, (block + 1) * tile_size)
        low_tile = meta[1 + seq * per_piece + block]
        high_tile = meta[0] * per_piece + block + 1
        query_first = (meta[0] * per_piece + block) * tile_size
        start_row = start_ref[0, :, span]

        def step(tile, carry):
            keys = keys_flat[pl.ds(pl.multiple_of(tile * tile_size, tile_size), tile_size), :]
            offset = pl.multiple_of((tile % per_piece) * tile_size, tile_size)
            values = value_ref[tile // per_piece, 0, :, pl.ds(offset, tile_size)]
            bias = tile_bias(tile, query_first, start_row)
            result = []
            for head in range(GROUP):
                run_max, run_total, run_acc = carry[head]
                scores = mm(keys, turned_ref[0, head * HD : (head + 1) * HD, span]) + bias
                new_max = jnp.maximum(run_max, jnp.max(scores, 0, keepdims=True))
                weights = jnp.exp(scores - new_max)
                factor = jnp.exp(run_max - new_max)
                new_total = run_total * factor + jnp.sum(weights, 0, keepdims=True)
                new_acc = run_acc * factor + mm(values, weights.astype(jnp.bfloat16))
                result.append((new_max, new_total, new_acc))
            return tuple(result)

        start = tuple(
            (
                jnp.full((1, tile_size), -1e30, jnp.float32),
                jnp.zeros((1, tile_size), jnp.float32),
                jnp.zeros((HD, tile_size), jnp.float32),
            )
            for _ in range(GROUP)
        )
        final = lax.fori_loop(low_tile, high_tile, step, start)
        for head in range(GROUP):
            run_max, run_total, run_acc = final[head]
            out_ref[0, head * HD : (head + 1) * HD, span] = (run_acc / run_total).astype(
                jnp.bfloat16
            )
            log_ref[0, 0, head : head + 1, span] = run_max + jnp.log(run_total)


def pull_kernel(
    meta, turned_ref, grad_ref, out_ref, log_ref, cos_ref, sin_ref, key_ref, value_ref, start_ref,
    query_back_ref, key_grad_ref, value_grad_ref,
    keys_flat, values_flat, key_sum, value_sum,
):
    seq = pl.program_id(0)
    pieces, rows = key_ref.shape[0], key_ref.shape[3]
    tile_size = tile_rows(rows)
    per_piece = rows // tile_size
    for piece in range(pieces):
        keys_flat[piece * rows : (piece + 1) * rows, :] = key_ref[piece, 0].T
        values_flat[piece * rows : (piece + 1) * rows, :] = value_ref[piece, 0].T
    key_sum[...] = jnp.zeros_like(key_sum)
    value_sum[...] = jnp.zeros_like(value_sum)
    for block in range(per_piece):
        span = slice(block * tile_size, (block + 1) * tile_size)
        low_tile = meta[1 + seq * per_piece + block]
        high_tile = meta[0] * per_piece + block + 1
        query_first = (meta[0] * per_piece + block) * tile_size
        start_row = start_ref[0, :, span]
        query_side, deltas = [], []
        for head in range(GROUP):
            query_cols = turned_ref[0, head * HD : (head + 1) * HD, span]
            grad_cols = grad_ref[0, head * HD : (head + 1) * HD, span]
            out_cols = out_ref[0, head * HD : (head + 1) * HD, span]
            deltas.append(
                jnp.sum(
                    grad_cols.astype(jnp.float32) * out_cols.astype(jnp.float32), 0, keepdims=True
                )
            )
            query_side.append((query_cols.T, grad_cols.T))

        def step(tile, carry):
            where = pl.ds(pl.multiple_of(tile * tile_size, tile_size), tile_size)
            keys = keys_flat[where, :]
            values = values_flat[where, :]
            offset = pl.multiple_of((tile % per_piece) * tile_size, tile_size)
            keys_across = key_ref[tile // per_piece, 0, :, pl.ds(offset, tile_size)]
            bias = tile_bias(tile, query_first, start_row)
            key_part = key_sum[where, :]
            value_part = value_sum[where, :]
            result = []
            for head in range(GROUP):
                rows_of = slice(head * HD, (head + 1) * HD)
                scores = mm(keys, turned_ref[0, rows_of, span]) + bias
                probs = jnp.exp(scores - log_ref[0, 0, head : head + 1, span])
                prob_grad = mm(values, grad_ref[0, rows_of, span])
                score_grad = (probs * (prob_grad - deltas[head])).astype(jnp.bfloat16)
                result.append(carry[head] + mm(keys_across, score_grad))
                key_part += mm(score_grad, query_side[head][0])
                value_part += mm(probs.astype(jnp.bfloat16), query_side[head][1])
            key_sum[where, :] = key_part
            value_sum[where, :] = value_part
            return tuple(result)

        final = lax.fori_loop(
            low_tile,
            high_tile,
            step,
            tuple(jnp.zeros((HD, tile_size), jnp.float32) for _ in range(GROUP)),
        )
        for head in range(GROUP):
            query_back_ref[0, head * HD : (head + 1) * HD, span] = turn(
                final[head] * (HD**-0.5), cos_ref[0, :, span], -sin_ref[0, :, span]
            ).astype(jnp.bfloat16)
    for piece in range(pieces):
        where = slice(piece * rows, (piece + 1) * rows)
        key_grad_ref[piece, 0] = key_sum[where, :].T.astype(jnp.bfloat16)
        value_grad_ref[piece, 0] = value_sum[where, :].T.astype(jnp.bfloat16)


def head_specs(pieces, rows):
    return dict(
        heads=pl.BlockSpec((1, GROUP * HD, rows), lambda s, g, m: (s, g, 0)),
        angle=pl.BlockSpec((1, HD // 2, rows), lambda s, g, m: (s, 0, 0)),
        key=pl.BlockSpec((pieces, 1, HD, rows), lambda s, g, m: (0, s, g, 0)),
        value=pl.BlockSpec((pieces, 1, HD, rows), lambda s, g, m: (0, s, KVH + g, 0)),
        start=pl.BlockSpec((1, 1, rows), lambda s, g, m: (s, 0, 0)),
        log=pl.BlockSpec((1, 1, GROUP, rows), lambda s, g, m: (s, g, 0, 0)),
    )


def attend(meta, query_raw, cosine, sine_part, pairs, doc_start):
    pieces, seqs, _, rows = pairs.shape
    spec = head_specs(pieces, rows)
    work = seqs * HQ * rows * rows * pieces * HD
    return pl.pallas_call(
        attend_kernel,
        grid_spec=pltpu.PrefetchScalarGridSpec(
            num_scalar_prefetch=1,
            grid=(seqs, KVH),
            in_specs=[
                spec["heads"], spec["angle"], spec["angle"], spec["key"], spec["value"],
                spec["start"],
            ],
            out_specs=[spec["heads"], spec["heads"], spec["log"]],
            scratch_shapes=[pltpu.VMEM((pieces * rows, HD), jnp.bfloat16)],
        ),
        out_shape=[
            jax.ShapeDtypeStruct((seqs, HQ * HD, rows), jnp.bfloat16),
            jax.ShapeDtypeStruct((seqs, HQ * HD, rows), jnp.bfloat16),
            jax.ShapeDtypeStruct((seqs, KVH, GROUP, rows), jnp.float32),
        ],
        compiler_params=pltpu.CompilerParams(vmem_limit_bytes=32 * 1024 * 1024),
        cost_estimate=pl.CostEstimate(
            flops=16 * work, bytes_accessed=32 * 1024 * 1024, transcendentals=work // HD
        ),
        name="attend",
    )(meta, query_raw, cosine, sine_part, pairs, pairs, doc_start)


def attend_pull(meta, turned, heads_grad, heads_out, log_total, cosine, sine_part, pairs, doc_start):
    pieces, seqs, _, rows = pairs.shape
    spec = head_specs(pieces, rows)
    work = seqs * HQ * rows * rows * pieces * HD
    return pl.pallas_call(
        pull_kernel,
        grid_spec=pltpu.PrefetchScalarGridSpec(
            num_scalar_prefetch=1,
            grid=(seqs, KVH),
            in_specs=[
                spec["heads"], spec["heads"], spec["heads"], spec["log"], spec["angle"],
                spec["angle"], spec["key"], spec["value"], spec["start"],
            ],
            out_specs=[spec["heads"], spec["key"], spec["key"]],
            scratch_shapes=[
                pltpu.VMEM((pieces * rows, HD), jnp.bfloat16),
                pltpu.VMEM((pieces * rows, HD), jnp.bfloat16),
                pltpu.VMEM((pieces * rows, HD), jnp.float32),
                pltpu.VMEM((pieces * rows, HD), jnp.float32),
            ],
        ),
        out_shape=[
            jax.ShapeDtypeStruct((seqs, HQ * HD, rows), jnp.bfloat16),
            jax.ShapeDtypeStruct((pieces, seqs, KVH * HD, rows), jnp.bfloat16),
            jax.ShapeDtypeStruct((pieces, seqs, KVH * HD, rows), jnp.bfloat16),
        ],
        compiler_params=pltpu.CompilerParams(vmem_limit_bytes=32 * 1024 * 1024),
        cost_estimate=pl.CostEstimate(
            flops=40 * work, bytes_accessed=48 * 1024 * 1024, transcendentals=work // HD
        ),
        name="attend_pull",
    )(meta, turned, heads_grad, heads_out, log_total, cosine, sine_part, pairs, pairs, doc_start)


def project_rows(left_side, weight):
    return jnp.einsum("sqd,de->sqe", left_side, weight, preferred_element_type=jnp.float32)


def project_across(left_side, weight):
    return jnp.einsum("sqd,de->seq", left_side, weight, preferred_element_type=jnp.float32)


def back_across(grad_rows, weight):
    return jnp.einsum("seq,de->sqd", grad_rows, weight, preferred_element_type=jnp.float32)


def weight_grad_across(left_side, grad_rows):
    return jnp.einsum("sqd,seq->de", left_side, grad_rows, preferred_element_type=jnp.float32)


def project_back(grad_rows, weight):
    return jnp.einsum("sqe,de->sqd", grad_rows, weight, preferred_element_type=jnp.float32)


def weight_grad(left_side, grad_rows):
    return jnp.einsum("sqd,sqe->de", left_side, grad_rows, preferred_element_type=jnp.float32)


def gated(gate_in, up_in):
    return jax.nn.silu(gate_in) * up_in


def body(
    tokens,
    positions,
    attn_gain,
    w_query,
    w_key,
    w_value,
    w_out,
    mlp_gain,
    w_gate,
    w_up,
    w_down,
    cotangent,
):
    seq_local = tokens.shape[0]
    rows_local = tokens.shape[1]
    shard = lax.axis_index("shard")
    query_index = shard * rows_local + jnp.arange(rows_local, dtype=jnp.int32)
    doc_start = query_index[None, :] - positions
    tile_size = tile_rows(rows_local)
    meta = jnp.concatenate(
        [
            jnp.reshape(shard, (1,)).astype(jnp.int32),
            jnp.reshape(doc_start[:, ::tile_size] // tile_size, (-1,)),
        ]
    )
    start_rows = doc_start[:, None, :]
    frequency = ROPE_BASE ** (-jnp.arange(HD // 2, dtype=jnp.float32) * 2.0 / HD)
    angles = positions.astype(jnp.float32)[:, None, :] * frequency[None, :, None]
    cosine, sine_part = jnp.cos(angles), jnp.sin(angles)
    full_query, full_key, full_value, full_out, first_gain = (
        lax.all_gather(w_query, "shard", axis=0, tiled=True),
        lax.all_gather(w_key, "shard", axis=0, tiled=True),
        lax.all_gather(w_value, "shard", axis=0, tiled=True),
        lax.all_gather(w_out, "shard", axis=0, tiled=True),
        lax.all_gather(attn_gain, "shard", axis=0, tiled=True),
    )
    tokens_wide = tokens.astype(jnp.float32)
    normed_one = normalize(tokens_wide, first_gain.astype(jnp.float32)).astype(jnp.bfloat16)
    key_rot = rotate_heads(project_across(normed_one, full_key), cosine, sine_part)
    value_rows = project_across(normed_one, full_value)
    pairs = lax.all_gather(
        jnp.concatenate([key_rot.astype(jnp.bfloat16), value_rows.astype(jnp.bfloat16)], 1),
        "shard",
        axis=0,
    )
    query_raw = project_across(normed_one, full_query)
    heads_out, query_rot, log_total = attend(
        meta, query_raw, cosine, sine_part, pairs, start_rows
    )
    mixed_rows = tokens_wide + jnp.einsum(
        "seq,ed->sqd", heads_out, full_out, preferred_element_type=jnp.float32
    )
    full_gate, full_up, full_down, second_gain = (
        lax.all_gather(w_gate, "shard", axis=0, tiled=True),
        lax.all_gather(w_up, "shard", axis=0, tiled=True),
        lax.all_gather(w_down, "shard", axis=0, tiled=True),
        lax.all_gather(mlp_gain, "shard", axis=0, tiled=True),
    )
    normed_two = normalize(mixed_rows, second_gain.astype(jnp.float32)).astype(jnp.bfloat16)
    gate_rows = project_rows(normed_two, full_gate).astype(jnp.bfloat16).astype(jnp.float32)
    up_rows = project_rows(normed_two, full_up).astype(jnp.bfloat16).astype(jnp.float32)
    hidden = gated(gate_rows, up_rows).astype(jnp.bfloat16)
    output = (mixed_rows + project_rows(hidden, full_down)).astype(jnp.bfloat16)
    hidden_grad = project_back(cotangent, full_down)
    gated_again, gated_pull = jax.vjp(gated, gate_rows, up_rows)
    gate_wide, up_wide = gated_pull(hidden_grad)
    gate_grad = gate_wide.astype(jnp.bfloat16)
    up_grad = up_wide.astype(jnp.bfloat16)
    normed_two_grad = project_back(gate_grad, full_gate) + project_back(up_grad, full_up)
    norm_again, norm_pull = jax.vjp(normalize, mixed_rows, second_gain.astype(jnp.float32))
    mixed_part, second_gain_grad = norm_pull(normed_two_grad)
    mixed_grad = cotangent.astype(jnp.float32) + mixed_part
    down_grad = weight_grad(hidden, cotangent)
    gate_weight_grad = weight_grad(normed_two, gate_grad)
    up_weight_grad = weight_grad(normed_two, up_grad)
    mlp_owned = (
        lax.psum_scatter(
            gate_weight_grad.astype(jnp.bfloat16), "shard", scatter_dimension=0, tiled=True
        ),
        lax.psum_scatter(
            up_weight_grad.astype(jnp.bfloat16), "shard", scatter_dimension=0, tiled=True
        ),
        lax.psum_scatter(
            down_grad.astype(jnp.bfloat16), "shard", scatter_dimension=0, tiled=True
        ),
        lax.psum_scatter(
            second_gain_grad.astype(jnp.bfloat16), "shard", scatter_dimension=0, tiled=True
        ),
    )
    mlp_summed = tuple(lax.psum(part, "dp") for part in mlp_owned)
    branch_grad = mixed_grad.astype(jnp.bfloat16)
    out_weight_grad = jnp.einsum(
        "seq,sqd->ed", heads_out, branch_grad, preferred_element_type=jnp.float32
    )
    heads_grad = jnp.einsum(
        "sqd,ed->seq", branch_grad, full_out, preferred_element_type=jnp.float32
    ).astype(jnp.bfloat16)
    query_back, key_grads, value_grads = attend_pull(
        meta, query_rot, heads_grad, heads_out, log_total, cosine, sine_part, pairs, start_rows
    )
    key_share = lax.psum_scatter(key_grads, "shard", scatter_dimension=0, tiled=False)
    value_back = lax.psum_scatter(value_grads, "shard", scatter_dimension=0, tiled=False)
    key_back = rotate_heads(key_share.astype(jnp.float32), cosine, -sine_part).astype(jnp.bfloat16)
    query_weight_grad = weight_grad_across(normed_one, query_back)
    key_weight_grad = weight_grad_across(normed_one, key_back)
    value_weight_grad = weight_grad_across(normed_one, value_back)
    normed_one_grad = (
        back_across(query_back, full_query)
        + back_across(key_back, full_key)
        + back_across(value_back, full_value)
    )
    first_again, first_pull = jax.vjp(normalize, tokens_wide, first_gain.astype(jnp.float32))
    token_part, first_gain_grad = first_pull(normed_one_grad)
    input_grad = mixed_grad + token_part
    attn_owned = (
        lax.psum_scatter(
            query_weight_grad.astype(jnp.bfloat16), "shard", scatter_dimension=0, tiled=True
        ),
        lax.psum_scatter(
            key_weight_grad.astype(jnp.bfloat16), "shard", scatter_dimension=0, tiled=True
        ),
        lax.psum_scatter(
            value_weight_grad.astype(jnp.bfloat16), "shard", scatter_dimension=0, tiled=True
        ),
        lax.psum_scatter(
            out_weight_grad.astype(jnp.bfloat16), "shard", scatter_dimension=0, tiled=True
        ),
        lax.psum_scatter(
            first_gain_grad.astype(jnp.bfloat16), "shard", scatter_dimension=0, tiled=True
        ),
    )
    attn_owned, mlp_summed = lax.optimization_barrier((attn_owned, mlp_summed))
    summed = tuple(lax.psum(part, "dp").astype(jnp.float32) for part in attn_owned) + tuple(
        part.astype(jnp.float32) for part in mlp_summed
    )
    return (
        output,
        input_grad,
        summed[4],
        summed[0],
        summed[1],
        summed[2],
        summed[3],
        summed[8],
        summed[5],
        summed[6],
        summed[7],
    )


def solution(mesh):
    in_specs = (
        P("dp", "shard", None),
        P("dp", "shard"),
        P("shard"),
        P("shard", None),
        P("shard", None),
        P("shard", None),
        P("shard", None),
        P("shard"),
        P("shard", None),
        P("shard", None),
        P("shard", None),
        P("dp", "shard", None),
    )
    out_specs = (
        P("dp", "shard", None),
        P("dp", "shard", None),
        P("shard"),
        P("shard", None),
        P("shard", None),
        P("shard", None),
        P("shard", None),
        P("shard"),
        P("shard", None),
        P("shard", None),
        P("shard", None),
    )
    return jax.shard_map(body, mesh=mesh, in_specs=in_specs, out_specs=out_specs, check_vma=False)
```

time: 1490 us -> 1260 us (0.85)
  matrix products: 641 us -> 244 us
  waiting for transfers between devices: 458 us -> 681 us
  other arithmetic: 229 us -> 48.9 us
  Pallas kernels: 0 us -> 133 us
  blocking collectives: 73.6 us -> 110 us
  local copies, waits for them, and re-layouts: 63.7 us -> 29.2 us
    dot_general x28 -> x12, matrix products: 391 us -> 75.9 us  [the longest x3 16.8 us: project_across(): jnp.einsum('sqd,de->seq', left_side, weight, preferred_element_type=jnp.f...]
    pallas_call x0 -> x2, Pallas kernels: none -> 133 us  [the longest x1 71.7 us: attend_pull(): pl.pallas_call(pull_kernel, grid_spec=pltpu.PrefetchScalarGridSpec(num_sc...]
    convert_element_type x15 -> x11, other arithmetic: 129 us -> 21.1 us  [the longest x4 10.7 us: body(): part.astype(jnp.float32)]
    psum x1 -> x2, waiting for transfers between devices: 120 us -> 195 us  [the longest x1 160 us: body(): mlp_summed = tuple((lax.psum(part, 'dp') for part in mlp_owned))]
    reduce_sum x4 -> x0, other arithmetic: 57 us -> none  [per_sequence(): new_total = run_total * factor + jnp.sum(weights, -1)]
    all_gather x1, waiting for transfers between devices: 0.01 us -> 49.7 us  [body(): lax.all_gather(w_gate, 'shard', axis=0, tiled=True)]
    all_gather x1, waiting for transfers between devices: 0.01 us -> 40.2 us  [body(): lax.all_gather(w_down, 'shard', axis=0, tiled=True)]
    reduce_scatter x2, waiting for transfers between devices: 72.1 us -> 110 us  [the longest x1 75.7 us: body(): lax.psum_scatter(value_grads, 'shard', scatter_dimension=0, tiled=False)]
  transfers between devices with their start and end apart: 17 -> 17, of which waited for: 9 -> 13; matrix products, arithmetic and copies ran while one was open for 28% -> 17% of each run, Pallas kernels for 0% -> 5%
where the time goes in v1:
time: 1260 us
  waiting for transfers between devices  681 us (54%)
  matrix products  244 us (19%)
  Pallas kernels  133 us (11%)
  blocking collectives  110 us (9%)
  other arithmetic  48.9 us (4%)
  local copies, waits for them, and re-layouts  29.2 us (2%)
  between operations  15.9 us (1%)
    psum x1, waiting for transfers between devices, body(): mlp_summed = tuple((lax.psum(part, 'dp') for part in mlp_owned))  160 us
    reduce_scatter x1, waiting for transfers between devices, body(): lax.psum_scatter(value_grads, 'shard', scatter_dimension=0, tiled=False)  75.7 us
    pallas_call x1, Pallas kernels, attend_pull(): pl.pallas_call(pull_kernel, grid_spec=pltpu.PrefetchScalarGridSpec(num_sc...  71.7 us
    dot_general x3, matrix products, project_rows(): jnp.einsum('sqd,de->sqe', left_side, weight, preferred_element_type=jnp.f...  67.4 us
    reduce_scatter x1, waiting for transfers between devices, body(): lax.psum_scatter(up_weight_grad.astype(jnp.bfloat16), 'shard', scatter_di...  65 us
    reduce_scatter x1, waiting for transfers between devices, body(): lax.psum_scatter(gate_weight_grad.astype(jnp.bfloat16), 'shard', scatter_...  64.9 us
    pallas_call x1, Pallas kernels, attend(): pl.pallas_call(attend_kernel, grid_spec=pltpu.PrefetchScalarGridSpec(num_...  61.3 us
    dot_general x3, matrix products, project_back(): jnp.einsum('sqe,de->sqd', grad_rows, weight, preferred_element_type=jnp.f...  53.7 us
  transfers between devices with their start and end apart: 17, of which 13 were waited for; matrix products, arithmetic and copies ran while one was open for 17% of the time, Pallas kernels for 5%

profile of v1, /device:TPU:0, one launch (start us, length us, event | category | flops | bytes accessed | tf_op | source)
XLA Modules:
  0.0 1263.4 jit_solution(3929489582966534417)
XLA Ops:
  18.3 17.1 %all-gather.1 = bf16[2,480,320]{1,2,0:T(8,128)(2,1)S(1)} all-gather(bf16[1,480,320]{1,2,0:T(8,128)(2,1)} %bitcast.118), channel_id=1, replica_groups=mesh['dp'=16,'shard'=2] {'shard'}, dimensions={0}, use_global_device_ids=true | all-gather | bytes 921600 | tf_op jit(solution)/shard_map/all_gather | solution.py:321
  36.7 17.5 %all-gather.2 = bf16[2,480,320]{1,2,0:T(8,128)(2,1)S(1)} all-gather(bf16[1,480,320]{1,2,0:T(8,128)(2,1)S(1)} %bitcast.119), channel_id=1, replica_groups=mesh['dp'=16,'shard'=2] {'shard'}, dimensions={0}, use_global_device_ids=true | all-gather | bytes 921600 | tf_op jit(solution)/shard_map/all_gather | solution.py:322
  72.5 11.3 convolution_bitcast_fusion.query_ref
  83.9 40.2 %all-gather.18.cloned.1.call-done = bf16[2560,960]{0,1:T(8,128)(2,1)} async-done(((bf16[1280,960]{0,1:T(8,128)(2,1)}), bf16[2560,960]{0,1:T(8,128)(2,1)}) %all-gather.18.cloned.1.call-update) | async-done | bytes 4915216 | tf_op jit(solution)/shard_map/all_gather | solution.py:345
  124.1 18.2 %fusion.15 = f32[4,512,2560]{2,1,0:T(8,128)} fusion(bf16[4,512,960]{1,2,0:T(8,128)(2,1)} %param.23, bf16[2560,960]{0,1:T(8,128)(2,1)} %all-gather.18.cloned.1.call-done), kind=kOutput, calls=%fused_computation.40 | convolution fusion | flops 10066329600 | bytes 29818880 | tf_op jit(solution)/shard_map/sqe,de->sqd/dot_general | solution.py:278
  142.3 52.5 %all-gather.20.cloned.1.call-done = bf16[8,640,512]{2,1,0:T(8,128)(2,1)} async-done(((bf16[4,640,512]{2,1,0:T(8,128)(2,1)}), bf16[8,640,512]{2,1,0:T(8,128)(2,1)}) %all-gather.20.cloned.1.call-update) | async-done | bytes 5242896 | tf_op jit(solution)/shard_map/all_gather | solution.py:330
  200.5 61.3 %attend.1 = (bf16[4,960,512]{2,1,0:T(8,128)(2,1)S(1)}, bf16[4,960,512]{2,1,0:T(8,128)(2,1)S(1)}, f32[4,5,3,512]{3,2,1,0:T(4,128)S(1)}) custom-call(s32[9]{0:T(128)S(1)} %pad_add_fusion.meta, f32[4,960,512]{2,1,0:T(8,128)S(1)} %copy-done.1, f32[4,32,512]{2,1,0:T(8,128)S(1)} %get-tuple-element.65.cos_ref, f32[4,32,512]{2,1,0:T(8,128)S(1)} %get-tuple-element.64.sin_ref, ...), custom_call_target="tpu_custom_call" | custom-call | flops 32212254720 | bytes 33554432 | tf_op jit(solution)/shard_map/attend/pallas_call | solution.py:202
  265.6 9.8 multiply_reduce_fusion.2
  281.3 12.9 %all-gather.16.cloned.1.call-done = bf16[960,2560]{1,0:T(8,128)(2,1)} async-done(((bf16[480,2560]{1,0:T(8,128)(2,1)}), bf16[960,2560]{1,0:T(8,128)(2,1)}) %all-gather.16.cloned.1.call-update) | async-done | bytes 4915216 | tf_op jit(solution)/shard_map/all_gather | solution.py:344
  294.2 16.6 %convolution_convert_fusion = bf16[4,512,2560]{2,1,0:T(8,128)(2,1)} fusion(bf16[4,512,960]{1,2,0:T(8,128)(2,1)} %multiply_convert_fusion.1, bf16[960,2560]{1,0:T(8,128)(2,1)} %all-gather.16.cloned.1.call-done), kind=kOutput, calls=%fused_computation.26 | convolution fusion | flops 10071572480 | bytes 19333120 | tf_op jit(solution)/shard_map/sqd,de->sqe/dot_general | solution.py:262
  310.9 49.7 %all-gather.14.cloned.1.call-done = bf16[960,2560]{1,0:T(8,128)(2,1)} async-done(((bf16[480,2560]{1,0:T(8,128)(2,1)}), bf16[960,2560]{1,0:T(8,128)(2,1)}) %all-gather.14.cloned.1.call-update) | async-done | bytes 4915216 | tf_op jit(solution)/shard_map/all_gather | solution.py:343
  360.6 33.7 %fusion.6 = (bf16[4,512,2560]{2,1,0:T(8,128)(2,1)}, bf16[4,512,2560]{2,1,0:T(8,128)(2,1)}, bf16[4,512,2560]{2,1,0:T(8,128)(2,1)}) fusion(f32[4,512,2560]{2,1,0:T(8,128)} %fusion.15, bf16[4,512,2560]{2,1,0:T(8,128)(2,1)} %convolution_convert_fusion, bf16[4,512,960]{1,2,0:T(8,128)(2,1)} %multiply_convert_fusion.1, ...), kind=kOutput, calls=%fused_computation.12 | convolution fusion | flops 10165944320 | bytes 71761920 | tf_op jit(solution)/shard_map/sqd,de->sqe/dot_general | solution.py:262
  394.2 16.6 %fusion.19 = f32[4,512,960]{1,2,0:T(8,128)} fusion(bf16[4,512,2560]{2,1,0:T(8,128)(2,1)} %get-tuple-element.57, bf16[960,2560]{1,0:T(8,128)(2,1)} %all-gather.16.cloned.1.call-done), kind=kOutput, calls=%fused_computation.44 | convolution fusion | flops 10066329600 | bytes 23265280 | tf_op jit(solution)/shard_map/sqe,de->sqd/dot_general | solution.py:278
  410.8 18.9 %multiply_reduce_fusion = (bf16[960]{0:T(1024)(128)(2,1)}, f32[4,512]{1,0:T(4,128)S(1)}, f32[4,512,960]{1,2,0:T(8,128)}) fusion(f32[4,512,960]{1,2,0:T(8,128)S(1)} %copy-done.12, f32[4,512]{1,0:T(4,128)S(1)} %fusion.44, f32[960]{0:T(1024)S(1)} %convert_element_type.137, f32[4,512,960]{1,2,0:T(8,128)} %fusion.19, ...), kind=kOutput, calls=%fused_computation.34 | convolution fusion | flops 10080089088 | bytes 39016064 | tf_op jit(solution)/shard_map/sqe,de->sqd/dot_general | solution.py:278
  445.7 71.7 %attend_pull.1 = (bf16[4,960,512]{2,1,0:T(8,128)(2,1)S(1)}, bf16[2,4,320,512]{3,2,1,0:T(8,128)(2,1)}, bf16[2,4,320,512]{3,2,1,0:T(8,128)(2,1)}) custom-call(s32[9]{0:T(128)S(1)} %pad_add_fusion.meta, bf16[4,960,512]{2,1,0:T(8,128)(2,1)S(1)} %copy-done.6, bf16[4,960,512]{2,1,0:T(8,128)(2,1)S(1)} %convert_bitcast_fusion.grad_ref, ...), custom_call_target="tpu_custom_call" | custom-call | flops 80530636800 | bytes 50331648 | tf_op jit(solution)/shard_map/attend_pull/pallas_call | solution.py:231
  520.2 15.6 %bitcast_convert_fusion = bf16[2560,960]{0,1:T(8,128)(2,1)} fusion(bf16[4,512,960]{1,2,0:T(8,128)(2,1)} %param.23, bf16[4,512,2560]{2,1,0:T(8,128)(2,1)} %get-tuple-element.58), kind=kOutput, calls=%fused_computation.21 | convolution fusion | flops 10068787200 | bytes 19333120 | tf_op jit(solution)/shard_map/sqd,sqe->de/dot_general | solution.py:282
  535.9 16.0 %bitcast_convert_fusion.2 = bf16[960,2560]{1,0:T(8,128)(2,1)} fusion(bf16[4,512,960]{1,2,0:T(8,128)(2,1)} %multiply_convert_fusion.1, bf16[4,512,2560]{2,1,0:T(8,128)(2,1)} %get-tuple-element.56), kind=kOutput, calls=%fused_computation.23 | convolution fusion | flops 10068787200 | bytes 19333120 | tf_op jit(solution)/shard_map/sqd,sqe->de/dot_general | solution.py:282
  552.0 15.6 %bitcast_convert_fusion.1 = bf16[960,2560]{1,0:T(8,128)(2,1)} fusion(bf16[4,512,960]{1,2,0:T(8,128)(2,1)} %multiply_convert_fusion.1, bf16[4,512,2560]{2,1,0:T(8,128)(2,1)} %get-tuple-element.57), kind=kOutput, calls=%fused_computation.22 | convolution fusion | flops 10068787200 | bytes 19333120 | tf_op jit(solution)/shard_map/sqd,sqe->de/dot_general | solution.py:282
  567.7 75.7 %reduce-scatter.16.cloned.1.call-done = bf16[1,4,320,512]{3,2,1,0:T(8,128)(2,1)} async-done(((bf16[2,4,320,512]{3,2,1,0:T(8,128)(2,1)}), bf16[1,4,320,512]{3,2,1,0:T(8,128)(2,1)}) %reduce-scatter.16.cloned.1.call-update) | async-done | bytes 1310736 | tf_op jit(solution)/shard_map/reduce_scatter | solution.py:391
  648.8 34.6 %reduce-scatter.14.cloned.1.call-done = bf16[1,4,320,512]{3,2,1,0:T(8,128)(2,1)} async-done(((bf16[2,4,320,512]{3,2,1,0:T(8,128)(2,1)}), bf16[1,4,320,512]{3,2,1,0:T(8,128)(2,1)}) %reduce-scatter.14.cloned.1.call-update) | async-done | bytes 1310736 | tf_op jit(solution)/shard_map/reduce_scatter | solution.py:390
  688.9 10.8 bitcast_convert_fusion.3
  708.9 39.5 %reduce-scatter.26.cloned.1.call-done = bf16[1280,960]{0,1:T(8,128)(2,1)} async-done(((bf16[2560,960]{0,1:T(8,128)(2,1)}), bf16[1280,960]{0,1:T(8,128)(2,1)}) %reduce-scatter.26.cloned.1.call-update) | async-done | bytes 2457616 | tf_op jit(solution)/shard_map/reduce_scatter | solution.py:372
  748.4 64.9 %reduce-scatter.22.cloned.1.call-done = bf16[480,2560]{1,0:T(8,128)(2,1)} async-done(((bf16[960,2560]{1,0:T(8,128)(2,1)}), bf16[480,2560]{1,0:T(8,128)(2,1)}) %reduce-scatter.22.cloned.1.call-update) | async-done | bytes 2457616 | tf_op jit(solution)/shard_map/reduce_scatter | solution.py:366
  813.3 65.0 %reduce-scatter.24.cloned.1.call-done = bf16[480,2560]{1,0:T(8,128)(2,1)} async-done(((bf16[960,2560]{1,0:T(8,128)(2,1)}), bf16[480,2560]{1,0:T(8,128)(2,1)}) %reduce-scatter.24.cloned.1.call-update) | async-done | bytes 2457616 | tf_op jit(solution)/shard_map/reduce_scatter | solution.py:369
  900.5 32.0 %psum.66 = bf16[480]{0:T(512)(128)(2,1)S(1)} all-reduce(bf16[480]{0:T(512)(128)(2,1)S(1)} %dynamic-slice.5), channel_id=1, replica_groups=mesh['dp'=16,'shard'=2] {'dp'}, use_global_device_ids=true, to_apply=%region_20.21 | all-reduce | flops 480 | bytes 1920 | tf_op jit(solution)/shard_map/psum | solution.py:379
  936.3 13.5 %reduce-scatter.20.cloned.1.call-done = bf16[480,960]{1,0:T(8,128)(2,1)} async-done(((bf16[960,960]{1,0:T(8,128)(2,1)}), bf16[480,960]{1,0:T(8,128)(2,1)}) %reduce-scatter.20.cloned.1.call-update) | async-done | bytes 921616 | tf_op jit(solution)/shard_map/reduce_scatter | solution.py:414
  949.8 33.2 %reduce-scatter.18.cloned.1.call-done = bf16[480,960]{1,0:T(8,128)(2,1)} async-done(((bf16[960,960]{1,0:T(8,128)(2,1)}), bf16[480,960]{1,0:T(8,128)(2,1)}) %reduce-scatter.18.cloned.1.call-update) | async-done | bytes 921616 | tf_op jit(solution)/shard_map/reduce_scatter | solution.py:405
  982.9 159.6 %all-reduce.13.cloned.1.call-done = (bf16[480,2560]{1,0:T(8,128)(2,1)}, bf16[480,2560]{1,0:T(8,128)(2,1)}, bf16[1280,960]{0,1:T(8,128)(2,1)}) async-done(((bf16[480,2560]{1,0:T(8,128)(2,1)}, bf16[480,2560]{1,0:T(8,128)(2,1)}, bf16[1280,960]{0,1:T(8,128)(2,1)}), (bf16[480,2560]{1,0:T(8,128)(2,1)}, bf16[480,2560]{1,0:T(8,128)(2,1)}, bf16[1280,960]{0,1:T(8,128)(2,1)})) %all-reduce.13.cloned.1.call-update) | async-done | bytes 7372816 | tf_op jit(solution)/shard_map/psum | solution.py:379
  1142.5 17.1 %add_convert_fusion = bf16[4,512,960]{1,2,0:T(8,128)(2,1)} fusion(f32[4,512,960]{1,2,0:T(8,128)} %copy-done.11, bf16[4,512,2560]{2,1,0:T(8,128)(2,1)} %get-tuple-element.58, bf16[2560,960]{0,1:T(8,128)(2,1)} %all-gather.18.cloned.1.call-done), kind=kOutput, calls=%fused_computation.37 | convolution fusion | flops 10070261760 | bytes 27197440 | tf_op jit(solution)/shard_map/sqd,de->sqe/dot_general | solution.py:262
  1159.6 9.1 fusion.12
  1168.7 32.8 %psum.67 = bf16[480]{0:T(512)(128)(2,1)S(1)} all-reduce(bf16[480]{0:T(512)(128)(2,1)S(1)} %dynamic-slice.3), channel_id=1, replica_groups=mesh['dp'=16,'shard'=2] {'dp'}, use_global_device_ids=true, to_apply=%region_21.22 | all-reduce | flops 480 | bytes 1920 | tf_op jit(solution)/shard_map/psum | solution.py:422
  1212.8 35.8 %all-reduce.11.cloned.1.call-done = (bf16[480,960]{1,0:T(8,128)(2,1)}, bf16[480,320]{0,1:T(8,128)(2,1)}, bf16[480,320]{0,1:T(8,128)(2,1)}, bf16[480,960]{1,0:T(8,128)(2,1)}) async-done(((bf16[480,960]{1,0:T(8,128)(2,1)}, bf16[480,320]{0,1:T(8,128)(2,1)}, bf16[480,320]{0,1:T(8,128)(2,1)}, bf16[480,960]{1,0:T(8,128)(2,1)}), (bf16[480,960]{1,0:T(8,128)(2,1)}, bf16[480,320]{0,1:T(8,128)(2,1)}, ...) | async-done | bytes 2457616 | tf_op jit(solution)/shard_map/psum | solution.py:422
  (163 shorter events, 128.7 us)
Async XLA Ops:
  7.2 29.6 %copy-start.22 = (bf16[480,320]{0,1:T(8,128)(2,1)S(1)}, bf16[480,320]{0,1:T(8,128)(2,1)}, u32[]{:S(2)}) copy-start(bf16[480,320]{0,1:T(8,128)(2,1)} %param.17) | copy-start | bytes 921604
  7.2 65.4 %all-gather.10.cloned.1.call-start = ((), (), s32[]{:S(2)}) async-start(), calls=%async_computation.9 | async-start | bytes 2949120 | tf_op jit(solution)/shard_map/all_gather | solution.py:320
  7.9 116.1 %all-gather.18.cloned.1.call-start = ((), (), s32[]{:S(2)}) async-start(), calls=%async_computation.13 | async-start | bytes 7372800 | tf_op jit(solution)/shard_map/all_gather | solution.py:345
  8.7 186.1 %all-gather.20.cloned.1.call-start = ((), (), s32[]{:S(2)}) async-start(), calls=%async_computation.21 | async-start | bytes 7864320 | tf_op jit(solution)/shard_map/all_gather | solution.py:330
  18.3 54.3 %copy-start.27 = (f32[960]{0:T(1024)}, f32[960]{0:T(1024)S(1)}, u32[]{:S(2)}) copy-start(f32[960]{0:T(1024)S(1)} %convert_element_type.131) | copy-start | bytes 11524
  35.4 23.3 %copy-start.29 = (s32[4,512]{1,0:T(4,128)S(1)}, s32[4,512]{1,0:T(4,128)}, u32[]{:S(2)}) copy-start(s32[4,512]{1,0:T(4,128)} %param.13) | copy-start | bytes 24580
  36.7 27.5 %copy-start.13 = (bf16[960,320,1]{0,1,2:T(8,128)(2,1)}, bf16[960,320,1]{0,1,2:T(8,128)(2,1)S(1)}, u32[]{:S(2)}) copy-start(bf16[960,320,1]{0,1,2:T(8,128)(2,1)S(1)} %reshape.114) | copy-start | bytes 1843204
  55.5 9.4 copy-start.15
  58.7 13.9 %copy-start.23 = (f32[4,512]{1,0:T(4,128)}, f32[4,512]{1,0:T(4,128)S(1)}, u32[]{:S(2)}) copy-start(f32[4,512]{1,0:T(4,128)S(1)} %fusion.43) | copy-start | bytes 24580
  70.3 195.3 %all-gather.12.cloned.1.call-start = ((), (), s32[]{:S(2)}) async-start(), calls=%async_computation.10 | async-start | bytes 2949120 | tf_op jit(solution)/shard_map/all_gather | solution.py:323
  70.9 223.3 %all-gather.16.cloned.1.call-start = ((), (), s32[]{:S(2)}) async-start(), calls=%async_computation.12 | async-start | bytes 7372800 | tf_op jit(solution)/shard_map/all_gather | solution.py:344
  71.5 289.1 %all-gather.14.cloned.1.call-start = ((), (), s32[]{:S(2)}) async-start(), calls=%async_computation.11 | async-start | bytes 7372800 | tf_op jit(solution)/shard_map/all_gather | solution.py:343
  72.0 571.3 %reduce-scatter.16.cloned.1.call-start = ((), (), s32[]{:S(2)}) async-start(), calls=%async_computation.15 | async-start | bytes 3932160 | tf_op jit(solution)/shard_map/reduce_scatter | solution.py:391
  394.2 16.6 %copy-start.12 = (f32[4,512,960]{1,2,0:T(8,128)S(1)}, f32[4,512,960]{1,2,0:T(8,128)}, u32[]{:S(2)}) copy-start(f32[4,512,960]{1,2,0:T(8,128)} %copy-done.11) | copy-start | bytes 23592964
  429.7 8.1 copy-start.32
  519.4 163.9 %reduce-scatter.14.cloned.1.call-start = ((), (), s32[]{:S(2)}) async-start(), calls=%async_computation.14 | async-start | bytes 3932160 | tf_op jit(solution)/shard_map/reduce_scatter | solution.py:390
  520.1 228.3 %reduce-scatter.26.cloned.1.call-start = ((), (), s32[]{:S(2)}) async-start(), calls=%async_computation.20 | async-start | bytes 7372800 | tf_op jit(solution)/shard_map/reduce_scatter | solution.py:372
  535.8 277.5 %reduce-scatter.22.cloned.1.call-start = ((), (), s32[]{:S(2)}) async-start(), calls=%async_computation.18 | async-start | bytes 7372800 | tf_op jit(solution)/shard_map/reduce_scatter | solution.py:366
  551.9 326.4 %reduce-scatter.24.cloned.1.call-start = ((), (), s32[]{:S(2)}) async-start(), calls=%async_computation.19 | async-start | bytes 7372800 | tf_op jit(solution)/shard_map/reduce_scatter | solution.py:369
  567.6 75.8 %copy-start.24 = (f32[4,512]{1,0:T(4,128)S(1)}, f32[4,512]{1,0:T(4,128)}, u32[]{:S(2)}) copy-start(f32[4,512]{1,0:T(4,128)} %copy-done.23) | copy-start | bytes 24580
  567.6 75.8 %copy-start.28 = (f32[960]{0:T(1024)S(1)}, f32[960]{0:T(1024)}, u32[]{:S(2)}) copy-start(f32[960]{0:T(1024)} %copy-done.27) | copy-start | bytes 11524
  567.6 364.9 %reduce-scatter.30.cloned.1.call-start = ((), (), s32[]{:S(2)}) async-start(), calls=%async_computation.23 | async-start | bytes 1105920
  647.5 37.6 %copy-start.20 = (f32[4,32,512]{2,1,0:T(8,128)S(1)}, f32[4,32,512]{2,1,0:T(8,128)}, u32[]{:S(2)}) copy-start(f32[4,32,512]{2,1,0:T(8,128)} %get-tuple-element.63) | copy-start | bytes 786436
  648.7 285.7 %reduce-scatter.28.cloned.1.call-start = ((), (), s32[]{:S(2)}) async-start(), calls=%async_computation.22 | async-start | bytes 1105920
  688.7 261.1 %reduce-scatter.20.cloned.1.call-start = ((), (), s32[]{:S(2)}) async-start(), calls=%async_computation.17 | async-start | bytes 2949120 | tf_op jit(solution)/shard_map/reduce_scatter | solution.py:414
  699.7 283.3 %reduce-scatter.18.cloned.1.call-start = ((), (), s32[]{:S(2)}) async-start(), calls=%async_computation.16 | async-start | bytes 2949120 | tf_op jit(solution)/shard_map/reduce_scatter | solution.py:405
  708.8 170.3 %copy-start.31 = (bf16[960,960]{1,0:T(8,128)(2,1)S(1)}, bf16[960,960]{1,0:T(8,128)(2,1)}, u32[]{:S(2)}) copy-start(bf16[960,960]{1,0:T(8,128)(2,1)} %all-gather.10.cloned.1.call-done) | copy-start | bytes 5529604
  708.8 433.7 %all-reduce.13.cloned.1.call-start = ((), (), s32[]{:S(2)}) async-start(), calls=%async_computation.25 | async-start | bytes 14745600 | tf_op jit(solution)/shard_map/psum | solution.py:379
  878.4 370.2 %all-reduce.11.cloned.1.call-start = ((), (), s32[]{:S(2)}) async-start(), calls=%async_computation.24 | async-start | bytes 5242880 | tf_op jit(solution)/shard_map/psum | solution.py:422
  1142.5 17.1 %copy-start.26 = (f32[4,512]{1,0:T(4,128)S(1)}, f32[4,512]{1,0:T(4,128)}, u32[]{:S(2)}) copy-start(f32[4,512]{1,0:T(4,128)} %copy-done.25) | copy-start | bytes 24580
  1142.5 17.1 %copy-start.10 = (bf16[4,512,960]{1,2,0:T(8,128)(2,1)S(1)}, bf16[4,512,960]{1,2,0:T(8,128)(2,1)}, u32[]{:S(2)}) copy-start(bf16[4,512,960]{1,2,0:T(8,128)(2,1)} %param.12) | copy-start | bytes 11796484
  1168.7 38.6 %copy-start.18 = (bf16[480,2560]{1,0:T(8,128)(2,1)S(1)}, bf16[480,2560]{1,0:T(8,128)(2,1)}, u32[]{:S(2)}) copy-start(bf16[480,2560]{1,0:T(8,128)(2,1)} %get-tuple-element.39) | copy-start | bytes 7372804
  (18 other events, 72.2 us)
Sparse Core Ops, SparseCore 0:
  9.6 46.5 all-gather.9
  57.7 66.3 all-gather.17
  126.2 68.5 all-gather.19
  196.2 31.6 all-gather.11
  229.2 64.9 all-gather.15
  295.6 64.9 all-gather.13
  519.5 123.8 reduce-scatter.15
  645.7 37.5 reduce-scatter.13
  686.2 62.1 reduce-scatter.25
  751.1 62.1 reduce-scatter.21
  816.2 62.0 reduce-scatter.23
  880.5 16.9 reduce-scatter.29
  899.7 16.9 reduce-scatter.27
  919.4 30.3 reduce-scatter.19
  952.5 30.3 reduce-scatter.17
  986.8 155.6 all-reduce.12
  1147.4 101.1 all-reduce.10

commit v2 on v1

--- a/solution.py
+++ b/solution.py
@@ -1,5 +1,3 @@
-import functools
-
 import jax
 import jax.numpy as jnp
 from jax import lax
@@ -282,6 +280,22 @@
     return jnp.einsum("sqd,sqe->de", left_side, grad_rows, preferred_element_type=jnp.float32)
 
 
+def scatter_sum(values):
+    count = lax.axis_size("shard")
+    index = lax.axis_index("shard")
+    size = values.shape[0] // count
+
+    def block(which):
+        return lax.dynamic_slice_in_dim(values, which * size, size, 0)
+
+    total = block(index).astype(jnp.float32)
+    for step in range(1, count):
+        order = [(source, (source + step) % count) for source in range(count)]
+        arrived = lax.ppermute(block((index + step) % count), "shard", order)
+        total += arrived.astype(jnp.float32)
+    return total
+
+
 def gated(gate_in, up_in):
     return jax.nn.silu(gate_in) * up_in
 
@@ -316,19 +330,23 @@
     frequency = ROPE_BASE ** (-jnp.arange(HD // 2, dtype=jnp.float32) * 2.0 / HD)
     angles = positions.astype(jnp.float32)[:, None, :] * frequency[None, :, None]
     cosine, sine_part = jnp.cos(angles), jnp.sin(angles)
-    full_query, full_key, full_value, full_out, first_gain = (
-        lax.all_gather(w_query, "shard", axis=0, tiled=True),
-        lax.all_gather(w_key, "shard", axis=0, tiled=True),
-        lax.all_gather(w_value, "shard", axis=0, tiled=True),
-        lax.all_gather(w_out, "shard", axis=0, tiled=True),
-        lax.all_gather(attn_gain, "shard", axis=0, tiled=True),
-    )
+    small = lax.all_gather(
+        jnp.concatenate([w_key, w_value, attn_gain[:, None], mlp_gain[:, None]], 1),
+        "shard",
+        axis=0,
+        tiled=True,
+    )
+    pair_width = 2 * KVH * HD
+    full_pair = small[:, :pair_width]
+    first_gain, second_gain = small[:, pair_width], small[:, pair_width + 1]
+    full_query = lax.all_gather(w_query, "shard", axis=0, tiled=True)
+    full_out = lax.all_gather(w_out, "shard", axis=0, tiled=True)
     tokens_wide = tokens.astype(jnp.float32)
     normed_one = normalize(tokens_wide, first_gain.astype(jnp.float32)).astype(jnp.bfloat16)
-    key_rot = rotate_heads(project_across(normed_one, full_key), cosine, sine_part)
-    value_rows = project_across(normed_one, full_value)
+    pair_rows = project_across(normed_one, full_pair)
+    key_rot = rotate_heads(pair_rows[:, : KVH * HD], cosine, sine_part)
     pairs = lax.all_gather(
-        jnp.concatenate([key_rot.astype(jnp.bfloat16), value_rows.astype(jnp.bfloat16)], 1),
+        jnp.concatenate([key_rot, pair_rows[:, KVH * HD :]], 1).astype(jnp.bfloat16),
         "shard",
         axis=0,
     )
@@ -339,11 +357,10 @@
     mixed_rows = tokens_wide + jnp.einsum(
         "seq,ed->sqd", heads_out, full_out, preferred_element_type=jnp.float32
     )
-    full_gate, full_up, full_down, second_gain = (
+    full_gate, full_up, full_down = (
         lax.all_gather(w_gate, "shard", axis=0, tiled=True),
         lax.all_gather(w_up, "shard", axis=0, tiled=True),
         lax.all_gather(w_down, "shard", axis=0, tiled=True),
-        lax.all_gather(mlp_gain, "shard", axis=0, tiled=True),
     )
     normed_two = normalize(mixed_rows, second_gain.astype(jnp.float32)).astype(jnp.bfloat16)
     gate_rows = project_rows(normed_two, full_gate).astype(jnp.bfloat16).astype(jnp.float32)
@@ -359,25 +376,18 @@
     norm_again, norm_pull = jax.vjp(normalize, mixed_rows, second_gain.astype(jnp.float32))
     mixed_part, second_gain_grad = norm_pull(normed_two_grad)
     mixed_grad = cotangent.astype(jnp.float32) + mixed_part
-    down_grad = weight_grad(hidden, cotangent)
-    gate_weight_grad = weight_grad(normed_two, gate_grad)
-    up_weight_grad = weight_grad(normed_two, up_grad)
-    mlp_owned = (
-        lax.psum_scatter(
-            gate_weight_grad.astype(jnp.bfloat16), "shard", scatter_dimension=0, tiled=True
-        ),
-        lax.psum_scatter(
-            up_weight_grad.astype(jnp.bfloat16), "shard", scatter_dimension=0, tiled=True
-        ),
-        lax.psum_scatter(
-            down_grad.astype(jnp.bfloat16), "shard", scatter_dimension=0, tiled=True
-        ),
-        lax.psum_scatter(
-            second_gain_grad.astype(jnp.bfloat16), "shard", scatter_dimension=0, tiled=True
-        ),
+    branch_grad = mixed_grad.astype(jnp.bfloat16)
+    down_grad = weight_grad(hidden, cotangent).astype(jnp.bfloat16)
+    gate_weight_grad = weight_grad(normed_two, gate_grad).astype(jnp.bfloat16)
+    up_weight_grad = weight_grad(normed_two, up_grad).astype(jnp.bfloat16)
+    down_grad, gate_weight_grad, up_weight_grad, branch_grad = lax.optimization_barrier(
+        (down_grad, gate_weight_grad, up_weight_grad, branch_grad)
+    )
+    mlp_owned = tuple(
+        scatter_sum(part).astype(jnp.bfloat16)
+        for part in (down_grad, gate_weight_grad, up_weight_grad)
     )
     mlp_summed = tuple(lax.psum(part, "dp") for part in mlp_owned)
-    branch_grad = mixed_grad.astype(jnp.bfloat16)
     out_weight_grad = jnp.einsum(
         "seq,sqd->ed", heads_out, branch_grad, preferred_element_type=jnp.float32
     )
@@ -387,53 +397,41 @@
     query_back, key_grads, value_grads = attend_pull(
         meta, query_rot, heads_grad, heads_out, log_total, cosine, sine_part, pairs, start_rows
     )
-    key_share = lax.psum_scatter(key_grads, "shard", scatter_dimension=0, tiled=False)
-    value_back = lax.psum_scatter(value_grads, "shard", scatter_dimension=0, tiled=False)
-    key_back = rotate_heads(key_share.astype(jnp.float32), cosine, -sine_part).astype(jnp.bfloat16)
+    key_share = scatter_sum(key_grads.reshape(-1, KVH * HD, rows_local))
+    value_share = scatter_sum(value_grads.reshape(-1, KVH * HD, rows_local))
+    pair_back = jnp.concatenate(
+        [rotate_heads(key_share, cosine, -sine_part), value_share], 1
+    ).astype(jnp.bfloat16)
     query_weight_grad = weight_grad_across(normed_one, query_back)
-    key_weight_grad = weight_grad_across(normed_one, key_back)
-    value_weight_grad = weight_grad_across(normed_one, value_back)
-    normed_one_grad = (
-        back_across(query_back, full_query)
-        + back_across(key_back, full_key)
-        + back_across(value_back, full_value)
-    )
+    pair_weight_grad = weight_grad_across(normed_one, pair_back)
+    normed_one_grad = back_across(query_back, full_query) + back_across(pair_back, full_pair)
     first_again, first_pull = jax.vjp(normalize, tokens_wide, first_gain.astype(jnp.float32))
     token_part, first_gain_grad = first_pull(normed_one_grad)
     input_grad = mixed_grad + token_part
-    attn_owned = (
-        lax.psum_scatter(
-            query_weight_grad.astype(jnp.bfloat16), "shard", scatter_dimension=0, tiled=True
-        ),
-        lax.psum_scatter(
-            key_weight_grad.astype(jnp.bfloat16), "shard", scatter_dimension=0, tiled=True
-        ),
-        lax.psum_scatter(
-            value_weight_grad.astype(jnp.bfloat16), "shard", scatter_dimension=0, tiled=True
-        ),
-        lax.psum_scatter(
-            out_weight_grad.astype(jnp.bfloat16), "shard", scatter_dimension=0, tiled=True
-        ),
-        lax.psum_scatter(
-            first_gain_grad.astype(jnp.bfloat16), "shard", scatter_dimension=0, tiled=True
-        ),
+    small_grad = jnp.concatenate(
+        [pair_weight_grad, first_gain_grad[:, None], second_gain_grad[:, None]], 1
+    )
+    attn_owned = tuple(
+        scatter_sum(part.astype(jnp.bfloat16)).astype(jnp.bfloat16)
+        for part in (out_weight_grad, query_weight_grad, small_grad)
     )
     attn_owned, mlp_summed = lax.optimization_barrier((attn_owned, mlp_summed))
-    summed = tuple(lax.psum(part, "dp").astype(jnp.float32) for part in attn_owned) + tuple(
-        part.astype(jnp.float32) for part in mlp_summed
-    )
+    out_sum, query_sum, small_sum = (
+        lax.psum(part, "dp").astype(jnp.float32) for part in attn_owned
+    )
+    down_sum, gate_sum, up_sum = (part.astype(jnp.float32) for part in mlp_summed)
     return (
         output,
         input_grad,
-        summed[4],
-        summed[0],
-        summed[1],
-        summed[2],
-        summed[3],
-        summed[8],
-        summed[5],
-        summed[6],
-        summed[7],
+        small_sum[:, pair_width],
+        query_sum,
+        small_sum[:, : KVH * HD],
+        small_sum[:, KVH * HD : pair_width],
+        out_sum,
+        small_sum[:, pair_width + 1],
+        gate_sum,
+        up_sum,
+        down_sum,
     )
 
 

time: 1260 us -> 1120 us (0.89); the launches traced: 1260 us -> 1110 us
  blocking collectives: 110 us -> 0 us
  waiting for transfers between devices: 681 us -> 579 us
  starting transfers between devices: 1.02 us -> 60.1 us
  matrix products: 244 us -> 219 us
  other arithmetic: 48.9 us -> 65.5 us
    reduce_scatter x7 -> x0, waiting for transfers between devices: 326 us -> none  [the longest x1 75.7 us: body(): lax.psum_scatter(value_grads, 'shard', scatter_dimension=0, tiled=False)]
    ppermute x0 -> x8, waiting for transfers between devices: none -> 164 us  [scatter_sum(): arrived = lax.ppermute(block((index + step) % count), 'shard', order)]
    psum x2 -> x0, blocking collectives: 64.9 us -> none  [the longest x1 32.8 us: body(): lax.psum(part, 'dp').astype(jnp.float32)]
    ppermute x0 -> x8, starting transfers between devices: none -> 59.7 us  [scatter_sum(): arrived = lax.ppermute(block((index + step) % count), 'shard', order)]
    all_gather x3 -> x4, waiting for transfers between devices: 52.5 us -> 101 us  [the longest x1 58.8 us: body(): lax.all_gather(jnp.concatenate([key_rot, pair_rows[:, KVH * HD:]], 1).ast...]
    psum x1, waiting for transfers between devices: 35.8 us -> 82.6 us  [body(): lax.psum(part, 'dp').astype(jnp.float32)]
    psum x1, waiting for transfers between devices: 160 us -> 116 us  [body(): mlp_summed = tuple((lax.psum(part, 'dp') for part in mlp_owned))]
    all_gather x2 -> x0, blocking collectives: 34.6 us -> none  [the longest x1 17.5 us: body(): lax.all_gather(w_value, 'shard', axis=0, tiled=True)]
  transfers between devices with their start and end apart: 17 -> 17, of which waited for: 13 -> 13; matrix products, arithmetic and copies ran while one was open for 17% -> 16% of each run, Pallas kernels for 5% -> 12%
where the time goes in v2:
time: 1120 us; the launch traced here: 1110 us
  waiting for transfers between devices  579 us (52%)
  matrix products  219 us (20%)
  Pallas kernels  133 us (12%)
  other arithmetic  65.5 us (6%)
  starting transfers between devices  60.1 us (5%)
  local copies, waits for them, and re-layouts  39 us (3%)
  between operations  15.1 us (1%)
    ppermute x8, waiting for transfers between devices, scatter_sum(): arrived = lax.ppermute(block((index + step) % count), 'shard', order)  164 us
    psum x1, waiting for transfers between devices, body(): mlp_summed = tuple((lax.psum(part, 'dp') for part in mlp_owned))  116 us
    psum x1, waiting for transfers between devices, body(): lax.psum(part, 'dp').astype(jnp.float32)  82.6 us
    pallas_call x1, Pallas kernels, attend_pull(): pl.pallas_call(pull_kernel, grid_spec=pltpu.PrefetchScalarGridSpec(num_sc...  71.2 us
    dot_general x3, matrix products, project_back(): jnp.einsum('sqe,de->sqd', grad_rows, weight, preferred_element_type=jnp.f...  65.7 us
    pallas_call x1, Pallas kernels, attend(): pl.pallas_call(attend_kernel, grid_spec=pltpu.PrefetchScalarGridSpec(num_...  61.5 us
    ppermute x8, starting transfers between devices, scatter_sum(): arrived = lax.ppermute(block((index + step) % count), 'shard', order)  59.7 us
    all_gather x1, waiting for transfers between devices, body(): lax.all_gather(jnp.concatenate([key_rot, pair_rows[:, KVH * HD:]], 1).ast...  58.8 us
  transfers between devices with their start and end apart: 17, of which 13 were waited for; matrix products, arithmetic and copies ran while one was open for 16% of the time, Pallas kernels for 12%

profile of v2, /device:TPU:0, one launch (start us, length us, event | category | flops | bytes accessed | tf_op | source)
XLA Modules:
  0.0 1109.9 jit_solution(11594473958461752164)
XLA Ops:
  16.2 21.7 %all-gather.21.cloned.1.call-done = bf16[2,480,642]{1,2,0:T(8,128)(2,1)} async-done(((bf16[1,480,642]{1,2,0:T(8,128)(2,1)}), bf16[2,480,642]{1,2,0:T(8,128)(2,1)}) %all-gather.21.cloned.1.call-update) | async-done | bytes 1232656 | tf_op jit(solution)/shard_map/all_gather | solution.py:333
  39.9 5.4 convolution_bitcast_fusion.1
  50.9 20.3 %all-gather.9.cloned.1.call-done = bf16[960,960]{1,0:T(8,128)(2,1)} async-done(((bf16[480,960]{1,0:T(8,128)(2,1)}), bf16[960,960]{1,0:T(8,128)(2,1)}) %all-gather.9.cloned.1.call-update) | async-done | bytes 1843216 | tf_op jit(solution)/shard_map/all_gather | solution.py:342
  71.1 11.9 %convolution_bitcast_fusion.query_ref = f32[4,960,512]{2,1,0:T(8,128)} fusion(bf16[960,960]{1,0:T(8,128)(2,1)} %all-gather.9.cloned.1.call-done, bf16[4,512,960]{1,2,0:T(8,128)(2,1)} %param.12, f32[960]{0:T(1024)S(1)} %get-tuple-element.83, f32[4,512]{1,0:T(4,128)S(1)} %fusion.37), kind=kOutput, calls=%fused_computation.55 | convolution fusion | flops 3782737920 | bytes 13651712 | tf_op jit(solution)/shard_map/sqd,de->seq/dot_general | solution.py:264
  83.1 58.8 %all-gather.11.cloned.1.call-done.key_ref.value_ref = bf16[2,4,640,512]{3,2,1,0:T(8,128)(2,1)} async-done(((bf16[1,4,640,512]{3,2,1,0:T(8,128)(2,1)}), bf16[2,4,640,512]{3,2,1,0:T(8,128)(2,1)}) %all-gather.11.cloned.1.call-update) | async-done | bytes 5242896 | tf_op jit(solution)/shard_map/all_gather | solution.py:348
  147.6 61.5 %attend.1 = (bf16[4,960,512]{2,1,0:T(8,128)(2,1)S(1)}, bf16[4,960,512]{2,1,0:T(8,128)(2,1)S(1)}, f32[4,5,3,512]{3,2,1,0:T(4,128)S(1)}) custom-call(s32[9]{0:T(128)S(1)} %pad_add_fusion.meta, f32[4,960,512]{2,1,0:T(8,128)S(1)} %copy-done.10, f32[4,32,512]{2,1,0:T(8,128)S(1)} %get-tuple-element.101.cos_ref, f32[4,32,512]{2,1,0:T(8,128)S(1)} %get-tuple-element.100.sin_ref, ...), custom_call_target="tpu_custom_call" | custom-call | flops 32212254720 | bytes 33554432 | tf_op jit(solution)/shard_map/attend/pallas_call | solution.py:200
  213.0 9.8 multiply_reduce_fusion.2
  228.6 12.6 %all-gather.17.cloned.1.call-done = bf16[960,2560]{1,0:T(8,128)(2,1)} async-done(((bf16[480,2560]{1,0:T(8,128)(2,1)}), bf16[960,2560]{1,0:T(8,128)(2,1)}) %all-gather.17.cloned.1.call-update) | async-done | bytes 4915216 | tf_op jit(solution)/shard_map/all_gather | solution.py:362
  241.3 16.8 %convolution_convert_fusion = bf16[4,512,2560]{2,1,0:T(8,128)(2,1)} fusion(bf16[4,512,960]{1,2,0:T(8,128)(2,1)} %multiply_convert_fusion.1, bf16[960,2560]{1,0:T(8,128)(2,1)} %all-gather.17.cloned.1.call-done), kind=kOutput, calls=%fused_computation.26 | convolution fusion | flops 10071572480 | bytes 19333120 | tf_op jit(solution)/shard_map/sqd,de->sqe/dot_general | solution.py:260
  258.1 49.5 %all-gather.15.cloned.1.call-done = bf16[960,2560]{1,0:T(8,128)(2,1)} async-done(((bf16[480,2560]{1,0:T(8,128)(2,1)}), bf16[960,2560]{1,0:T(8,128)(2,1)}) %all-gather.15.cloned.1.call-update) | async-done | bytes 4915216 | tf_op jit(solution)/shard_map/all_gather | solution.py:361
  307.6 16.7 %convolution_convert_fusion.1 = bf16[4,512,2560]{2,1,0:T(8,128)(2,1)} fusion(bf16[4,512,960]{1,2,0:T(8,128)(2,1)} %multiply_convert_fusion.1, bf16[960,2560]{1,0:T(8,128)(2,1)} %all-gather.15.cloned.1.call-done), kind=kOutput, calls=%fused_computation.27 | convolution fusion | flops 10071572480 | bytes 19333120 | tf_op jit(solution)/shard_map/sqd,de->sqe/dot_general | solution.py:260
  324.3 49.8 %all-gather.19.cloned.1.call-done = bf16[2560,960]{0,1:T(8,128)(2,1)} async-done(((bf16[1280,960]{0,1:T(8,128)(2,1)}), bf16[2560,960]{0,1:T(8,128)(2,1)}) %all-gather.19.cloned.1.call-update) | async-done | bytes 4915216 | tf_op jit(solution)/shard_map/all_gather | solution.py:363
  374.1 30.8 %multiply_convert_fusion = (bf16[4,512,2560]{2,1,0:T(8,128)(2,1)S(1)}, bf16[4,512,2560]{2,1,0:T(8,128)(2,1)}, bf16[4,512,2560]{2,1,0:T(8,128)(2,1)}) fusion(bf16[4,512,2560]{2,1,0:T(8,128)(2,1)} %convolution_convert_fusion.1, bf16[4,512,2560]{2,1,0:T(8,128)(2,1)} %convolution_convert_fusion, bf16[4,512,960]{1,2,0:T(8,128)(2,1)} %param.23, ...), kind=kOutput, calls=%fused_computation.13 | convolution fusion | flops 10160701440 | bytes 61276160 | tf_op jit(solution)/shard_map/sqe,de->sqd/dot_general | solution.py:276
  404.9 11.8 %bitcast_convert_fusion = bf16[960,2560]{1,0:T(8,128)(2,1)} fusion(bf16[4,512,960]{1,2,0:T(8,128)(2,1)S(1)} %copy-done.20, bf16[4,512,2560]{2,1,0:T(8,128)(2,1)S(1)} %get-tuple-element.90), kind=kOutput, calls=%fused_computation.21 | convolution fusion | flops 10068787200 | bytes 19333120 | tf_op jit(solution)/shard_map/sqd,sqe->de/dot_general | solution.py:280
  416.7 14.6 %bitcast_convert_fusion.1 = bf16[960,2560]{1,0:T(8,128)(2,1)} fusion(bf16[4,512,960]{1,2,0:T(8,128)(2,1)S(1)} %copy-done.20, bf16[4,512,2560]{2,1,0:T(8,128)(2,1)} %get-tuple-element.91), kind=kOutput, calls=%fused_computation.22 | convolution fusion | flops 10068787200 | bytes 19333120 | tf_op jit(solution)/shard_map/sqd,sqe->de/dot_general | solution.py:280
  431.3 15.7 %fusion.19 = f32[4,512,960]{1,2,0:T(8,128)} fusion(bf16[4,512,2560]{2,1,0:T(8,128)(2,1)} %copy-done.53, bf16[960,2560]{1,0:T(8,128)(2,1)S(1)} %bitcast.112), kind=kOutput, calls=%fused_computation.43 | convolution fusion | flops 10066329600 | bytes 23265280 | tf_op jit(solution)/shard_map/sqe,de->sqd/dot_general | solution.py:276
  447.0 19.3 %multiply_reduce_fusion = (bf16[960]{0:T(1024)(128)(2,1)}, f32[4,512]{1,0:T(4,128)S(1)}, f32[4,512,960]{1,2,0:T(8,128)}) fusion(f32[4,512,960]{1,2,0:T(8,128)S(1)} %bitcast.96, f32[4,512]{1,0:T(4,128)S(1)} %copy-done.33, f32[960]{0:T(1024)S(1)} %copy-done.40, f32[4,512,960]{1,2,0:T(8,128)} %fusion.19, bf16[4,512,2560]{2,1,0:T(8,128)(2,1)} %get-tuple-element.91, ...), kind=kOutput, calls=%fused_computation.34 | convolution fusion | flops 10080089088 | bytes 39016064 | tf_op jit(solution)/shard_map/sqe,de->sqd/dot_general | solution.py:276
  466.3 15.8 %bitcast_convert_fusion.2 = bf16[2560,960]{0,1:T(8,128)(2,1)} fusion(bf16[4,512,960]{1,2,0:T(8,128)(2,1)} %param.23, bf16[4,512,2560]{2,1,0:T(8,128)(2,1)} %get-tuple-element.92), kind=kOutput, calls=%fused_computation.23 | convolution fusion | flops 10068787200 | bytes 19333120 | tf_op jit(solution)/shard_map/sqd,sqe->de/dot_general | solution.py:280
  482.1 4.5 fusion.43
  486.6 6.5 bitcast_convert_fusion.4
  500.5 71.2 %attend_pull.1 = (bf16[4,960,512]{2,1,0:T(8,128)(2,1)S(1)}, bf16[2,4,320,512]{3,2,1,0:T(8,128)(2,1)S(1)}, bf16[2,4,320,512]{3,2,1,0:T(8,128)(2,1)S(1)}) custom-call(s32[9]{0:T(128)S(1)} %copy-done.9, bf16[4,960,512]{2,1,0:T(8,128)(2,1)S(1)} %copy-done.14, bf16[4,960,512]{2,1,0:T(8,128)(2,1)S(1)} %convert_bitcast_fusion.grad_ref, ...), custom_call_target="tpu_custom_call" | custom-call | flops 80530636800 | bytes 50331648 | tf_op jit(solution)/shard_map/attend_pull/pallas_call | solution.py:229
  572.9 51.0 %collective-permute-start = (bf16[4,320,512]{2,1,0:T(8,128)(2,1)}, bf16[4,320,512]{2,1,0:T(8,128)(2,1)}, u32[]{:S(2)}, u32[]{:S(2)}) collective-permute-start(bf16[4,320,512]{2,1,0:T(8,128)(2,1)} %constant_dynamic-slice_fusion.7), channel_id=1, source_target_pairs={{0,1},{1,0},{2,3},{3,2},{4,5},{5,4},{6,7},{7,6},{8,9},{9,8},{10,11... | collective-permute-start | bytes 3932168 | tf_op jit(solution)/shard_map/ppermute | solution.py:294
  632.5 16.0 %add_convert_fusion = bf16[4,512,960]{1,2,0:T(8,128)(2,1)} fusion(f32[4,512,960]{1,2,0:T(8,128)S(1)} %bitcast.96, bf16[4,512,2560]{2,1,0:T(8,128)(2,1)} %get-tuple-element.92, bf16[2560,960]{0,1:T(8,128)(2,1)} %all-gather.19.cloned.1.call-done), kind=kOutput, calls=%fused_computation.36 | convolution fusion | flops 10070261760 | bytes 27197440 | tf_op jit(solution)/shard_map/sqd,de->sqe/dot_general | solution.py:260
  658.3 6.5 fusion.32
  664.7 41.8 %collective-permute-done.7 = bf16[480,2560]{1,0:T(8,128)(2,1)} collective-permute-done((bf16[480,2560]{1,0:T(8,128)(2,1)}, bf16[480,2560]{1,0:T(8,128)(2,1)}, u32[]{:S(2)}, u32[]{:S(2)}) %collective-permute-start.7) | collective-permute-done | bytes 2457632 | tf_op jit(solution)/shard_map/ppermute | solution.py:294
  712.3 46.9 %collective-permute-done.5 = bf16[1280,960]{0,1:T(8,128)(2,1)} collective-permute-done((bf16[1280,960]{0,1:T(8,128)(2,1)}, bf16[1280,960]{0,1:T(8,128)(2,1)}, u32[]{:S(2)}, u32[]{:S(2)}) %collective-permute-start.5) | collective-permute-done | bytes 2457632 | tf_op jit(solution)/shard_map/ppermute | solution.py:294
  765.0 46.7 %collective-permute-done.6 = bf16[480,2560]{1,0:T(8,128)(2,1)S(1)} collective-permute-done((bf16[480,2560]{1,0:T(8,128)(2,1)S(1)}, bf16[480,2560]{1,0:T(8,128)(2,1)S(1)}, u32[]{:S(2)}, u32[]{:S(2)}) %collective-permute-start.6) | collective-permute-done | bytes 2457632 | tf_op jit(solution)/shard_map/ppermute | solution.py:294
  813.9 26.0 %collective-permute-done.1 = bf16[4,320,512]{2,1,0:T(8,128)(2,1)} collective-permute-done((bf16[4,320,512]{2,1,0:T(8,128)(2,1)}, bf16[4,320,512]{2,1,0:T(8,128)(2,1)}, u32[]{:S(2)}, u32[]{:S(2)}) %collective-permute-start.1) | collective-permute-done | bytes 1310752 | tf_op jit(solution)/shard_map/ppermute | solution.py:294
  845.4 9.4 fusion.10
  870.9 116.5 %all-reduce.7.cloned.1.call-done = (bf16[1280,960]{0,1:T(8,128)(2,1)}, bf16[480,2560]{1,0:T(8,128)(2,1)}, bf16[480,2560]{1,0:T(8,128)(2,1)}) async-done(((bf16[1280,960]{0,1:T(8,128)(2,1)}, bf16[480,2560]{1,0:T(8,128)(2,1)}, bf16[480,2560]{1,0:T(8,128)(2,1)}), (bf16[1280,960]{0,1:T(8,128)(2,1)}, bf16[480,2560]{1,0:T(8,128)(2,1)}, bf16[480,2560]{1,0:T(8,128)(2,1)})) %all-reduce.7.cloned.1.call-update) | async-done | bytes 7372816 | tf_op jit(solution)/shard_map/psum | solution.py:390
  987.4 15.8 %fusion.12 = f32[4,512,960]{1,2,0:T(8,128)} fusion(bf16[4,512,960]{1,2,0:T(8,128)(2,1)} %param.12, f32[4,512,960]{1,2,0:T(8,128)} %get-tuple-element.107, f32[4,512]{1,0:T(4,128)S(1)} %copy-done.41, f32[960]{0:T(1024)} %copy-done.46, f32[4,512]{1,0:T(4,128)} %copy-done.42, f32[4,512,960]{1,2,0:T(8,128)} %copy-done.15, f32[4,512]{1,0:T(4,128)S(1)} %copy-done.36, ...), kind=kLoop, calls=%fused_computation.31 | loop fusion | flops 27525120 | bytes 39362048 | tf_op jit(solution)/shard_map/add | solution.py:410
  1011.6 82.6 %all-reduce.5.cloned.1.call-done = (bf16[480,642]{1,0:T(8,128)(2,1)}, bf16[480,960]{1,0:T(8,128)(2,1)}, bf16[480,960]{1,0:T(8,128)(2,1)}) async-done(((bf16[480,642]{1,0:T(8,128)(2,1)}, bf16[480,960]{1,0:T(8,128)(2,1)}, bf16[480,960]{1,0:T(8,128)(2,1)}), (bf16[480,642]{1,0:T(8,128)(2,1)}, bf16[480,960]{1,0:T(8,128)(2,1)}, bf16[480,960]{1,0:T(8,128)(2,1)})) %all-reduce.5.cloned.1.call-update) | async-done | bytes 2459536 | tf_op jit(solution)/shard_map/psum | solution.py:420
  (223 shorter events, 110.8 us)
Async XLA Ops:
  7.2 30.7 %all-gather.21.cloned.1.call-start = ((), (), s32[]{:S(2)}) async-start(), calls=%async_computation.6 | async-start | bytes 1990656 | tf_op jit(solution)/shard_map/all_gather | solution.py:333
  10.6 60.5 %all-gather.9.cloned.1.call-start = ((), (), s32[]{:S(2)}) async-start(), calls=%async_computation | async-start | bytes 2949120 | tf_op jit(solution)/shard_map/all_gather | solution.py:342
  11.4 130.5 %all-gather.11.cloned.1.call-start = ((), (), s32[]{:S(2)}) async-start(), calls=%async_computation.1 | async-start | bytes 7864320 | tf_op jit(solution)/shard_map/all_gather | solution.py:348
  16.2 125.7 %copy-start.1 = (f32[4,32,512]{2,1,0:T(8,128)}, f32[4,32,512]{2,1,0:T(8,128)S(1)}, u32[]{:S(2)}) copy-start(f32[4,32,512]{2,1,0:T(8,128)S(1)} %get-tuple-element.101.cos_ref) | copy-start | bytes 786436
  16.2 125.7 %copy-start.3 = (f32[4,32,512]{2,1,0:T(8,128)}, f32[4,32,512]{2,1,0:T(8,128)S(1)}, u32[]{:S(2)}) copy-start(f32[4,32,512]{2,1,0:T(8,128)S(1)} %get-tuple-element.100.sin_ref) | copy-start | bytes 786436
  16.2 55.0 %copy-start.42 = (f32[4,512]{1,0:T(4,128)}, f32[4,512]{1,0:T(4,128)S(1)}, u32[]{:S(2)}) copy-start(f32[4,512]{1,0:T(4,128)S(1)} %fusion.37) | copy-start | bytes 24580
  39.9 182.9 %copy-start.39 = (f32[960]{0:T(1024)}, f32[960]{0:T(1024)S(1)}, u32[]{:S(2)}) copy-start(f32[960]{0:T(1024)S(1)} %get-tuple-element.82) | copy-start | bytes 11524
  48.0 164.9 %all-gather.13.cloned.1.call-start = ((), (), s32[]{:S(2)}) async-start(), calls=%async_computation.2 | async-start | bytes 2949120 | tf_op jit(solution)/shard_map/all_gather | solution.py:343
  48.6 192.7 %all-gather.17.cloned.1.call-start = ((), (), s32[]{:S(2)}) async-start(), calls=%async_computation.4 | async-start | bytes 7372800 | tf_op jit(solution)/shard_map/all_gather | solution.py:362
  49.2 258.4 %all-gather.15.cloned.1.call-start = ((), (), s32[]{:S(2)}) async-start(), calls=%async_computation.3 | async-start | bytes 7372800 | tf_op jit(solution)/shard_map/all_gather | solution.py:361
  49.8 324.3 %all-gather.19.cloned.1.call-start = ((), (), s32[]{:S(2)}) async-start(), calls=%async_computation.5 | async-start | bytes 7372800 | tf_op jit(solution)/shard_map/all_gather | solution.py:363
  50.5 936.8 %all-reduce.7.cloned.1.call-start = ((), (), s32[]{:S(2)}) async-start(), calls=%async_computation.8 | async-start | bytes 14745600 | tf_op jit(solution)/shard_map/psum | solution.py:390
  50.7 91.2 %copy-start.5 = (s32[4,1,512]{2,1,0:T(1,128)}, s32[4,1,512]{2,1,0:T(1,128)S(1)}, u32[]{:S(2)}) copy-start(s32[4,1,512]{2,1,0:T(1,128)S(1)} %broadcast_in_dim.18.start_ref) | copy-start | bytes 24580
  50.9 91.0 %copy-start.8 = (s32[9]{0:T(128)}, s32[9]{0:T(128)S(1)}, u32[]{:S(2)}) copy-start(s32[9]{0:T(128)S(1)} %pad_add_fusion.meta) | copy-start | bytes 112
  495.5 365.4 %collective-permute-start.2 = (bf16[480,960]{1,0:T(8,128)(2,1)}, bf16[480,960]{1,0:T(8,128)(2,1)}, u32[]{:S(2)}, u32[]{:S(2)}) collective-permute-start(bf16[480,960]{1,0:T(8,128)(2,1)} %constant_dynamic-slice_fusion.5), channel_id=1, source_target_pairs={{0,1},{1,0},{2,3},{3,2},{4,5},{5,4},{6,7},{7,6},{8,9},{9,8},{10,11... | collective-permute-start | bytes 2764808 | tf_op jit(solution)/shard_map/ppermute | solution.py:294
  571.6 84.2 %copy-start = (bf16[2,4,320,512]{3,2,1,0:T(8,128)(2,1)}, bf16[2,4,320,512]{3,2,1,0:T(8,128)(2,1)S(1)}, u32[]{:S(2)}) copy-start(bf16[2,4,320,512]{3,2,1,0:T(8,128)(2,1)S(1)} %get-tuple-element.33) | copy-start | bytes 7864324
  572.9 241.0 %collective-permute-start = (bf16[4,320,512]{2,1,0:T(8,128)(2,1)}, bf16[4,320,512]{2,1,0:T(8,128)(2,1)}, u32[]{:S(2)}, u32[]{:S(2)}) collective-permute-start(bf16[4,320,512]{2,1,0:T(8,128)(2,1)} %constant_dynamic-slice_fusion.7), channel_id=1, source_target_pairs={{0,1},{1,0},{2,3},{3,2},{4,5},{5,4},{6,7},{7,6},{8,9},{9,8},{10,11... | collective-permute-start | bytes 3932168 | tf_op jit(solution)/shard_map/ppermute | solution.py:294
  627.1 79.4 %collective-permute-start.7 = (bf16[480,2560]{1,0:T(8,128)(2,1)}, bf16[480,2560]{1,0:T(8,128)(2,1)}, u32[]{:S(2)}, u32[]{:S(2)}) collective-permute-start(bf16[480,2560]{1,0:T(8,128)(2,1)} %constant_dynamic-slice_fusion), channel_id=1, source_target_pairs={{0,1},{1,0},{2,3},{3,2},{4,5},{5,4},{6,7},{7,6},{8,9},{9,8},{10,11... | collective-permute-start | bytes 7372808 | tf_op jit(solution)/shard_map/ppermute | solution.py:294
  630.6 128.6 %collective-permute-start.5 = (bf16[1280,960]{0,1:T(8,128)(2,1)}, bf16[1280,960]{0,1:T(8,128)(2,1)}, u32[]{:S(2)}, u32[]{:S(2)}) collective-permute-start(bf16[1280,960]{0,1:T(8,128)(2,1)} %constant_dynamic-slice_fusion.2), channel_id=1, source_target_pairs={{0,1},{1,0},{2,3},{3,2},{4,5},{5,4},{6,7},{7,6},{8,9},{9,8},{10,11... | collective-permute-start | bytes 7372808 | tf_op jit(solution)/shard_map/ppermute | solution.py:294
  652.9 55.6 %slice-start.4 = ((s8[4915200]{0:T(1024)(128)(4,1)}), s8[4194304]{0:T(1024)(128)(4,1)S(1)}, s32[]{:S(2)}) async-start(s8[4915200]{0:T(1024)(128)(4,1)} %bitcast.102), calls=%async_computation.13 | async-start | bytes 8388608
  652.9 158.8 %slice-start.2 = ((s8[4915200]{0:T(1024)(128)(4,1)}), s8[4194304]{0:T(1024)(128)(4,1)S(1)}, s32[]{:S(2)}) async-start(s8[4915200]{0:T(1024)(128)(4,1)} %bitcast.100), calls=%async_computation.11 | async-start | bytes 8388608
  655.5 156.2 %collective-permute-start.6 = (bf16[480,2560]{1,0:T(8,128)(2,1)S(1)}, bf16[480,2560]{1,0:T(8,128)(2,1)S(1)}, u32[]{:S(2)}, u32[]{:S(2)}) collective-permute-start(bf16[480,2560]{1,0:T(8,128)(2,1)S(1)} %constant_dynamic-slice_fusion.1), channel_id=1, source_target_pairs={{0,1},{1,0},{2,3},{3,2},{4,5},{5,4},{6,7},{7,6},{8,9},{9,8},{10,11... | collective-permute-start | bytes 7372808 | tf_op jit(solution)/shard_map/ppermute | solution.py:294
  658.0 103.2 %slice-start.6 = ((s8[4915200]{0:T(1024)(128)(4,1)}), s8[4194304]{0:T(1024)(128)(4,1)S(1)}, s32[]{:S(2)}) async-start(s8[4915200]{0:T(1024)(128)(4,1)} %bitcast.104), calls=%async_computation.15 | async-start | bytes 8388608
  658.2 103.0 %slice-start.7 = ((s8[4915200]{0:T(1024)(128)(4,1)}), s8[720896]{0:T(1024)(128)(4,1)S(1)}, s32[]{:S(2)}) async-start(s8[4915200]{0:T(1024)(128)(4,1)} %bitcast.104), calls=%async_computation.16 | async-start | bytes 1441792
  658.2 153.5 %slice-start.3 = ((s8[4915200]{0:T(1024)(128)(4,1)}), s8[720896]{0:T(1024)(128)(4,1)S(1)}, s32[]{:S(2)}) async-start(s8[4915200]{0:T(1024)(128)(4,1)} %bitcast.100), calls=%async_computation.12 | async-start | bytes 1441792
  706.5 133.4 %collective-permute-start.1 = (bf16[4,320,512]{2,1,0:T(8,128)(2,1)}, bf16[4,320,512]{2,1,0:T(8,128)(2,1)}, u32[]{:S(2)}, u32[]{:S(2)}) collective-permute-start(bf16[4,320,512]{2,1,0:T(8,128)(2,1)} %constant_dynamic-slice_fusion.6), channel_id=1, source_target_pairs={{0,1},{1,0},{2,3},{3,2},{4,5},{5,4},{6,7},{7,6},{8,9},{9,8},{10,11... | collective-permute-start | bytes 3932168 | tf_op jit(solution)/shard_map/ppermute | solution.py:294
  759.2 104.6 %collective-permute-start.3 = (bf16[480,960]{1,0:T(8,128)(2,1)}, bf16[480,960]{1,0:T(8,128)(2,1)}, u32[]{:S(2)}, u32[]{:S(2)}) collective-permute-start(bf16[480,960]{1,0:T(8,128)(2,1)} %constant_dynamic-slice_fusion.4), channel_id=1, source_target_pairs={{0,1},{1,0},{2,3},{3,2},{4,5},{5,4},{6,7},{7,6},{8,9},{9,8},{10,11... | collective-permute-start | bytes 2764808 | tf_op jit(solution)/shard_map/ppermute | solution.py:294
  813.8 280.3 %all-reduce.5.cloned.1.call-start = ((), (), s32[]{:S(2)}) async-start(), calls=%async_computation.7 | async-start | bytes 5406720 | tf_op jit(solution)/shard_map/psum | solution.py:420
  858.8 10.7 collective-permute-start.4
  863.7 123.7 %copy-start.34 = (f32[4,512]{1,0:T(4,128)S(1)}, f32[4,512]{1,0:T(4,128)}, u32[]{:S(2)}) copy-start(f32[4,512]{1,0:T(4,128)} %copy-done.32) | copy-start | bytes 24580
  863.7 123.7 %copy-start.36 = (f32[4,512]{1,0:T(4,128)S(1)}, f32[4,512]{1,0:T(4,128)}, u32[]{:S(2)}) copy-start(f32[4,512]{1,0:T(4,128)} %copy-done.35) | copy-start | bytes 24580
  869.5 117.8 %copy-start.41 = (f32[4,512]{1,0:T(4,128)S(1)}, f32[4,512]{1,0:T(4,128)}, u32[]{:S(2)}) copy-start(f32[4,512]{1,0:T(4,128)} %multiply_multiply_fusion) | copy-start | bytes 24580
  (49 other events, 548.1 us)
Sparse Core Ops, SparseCore 0:
  10.7 27.1 all-gather.20
  39.5 31.6 all-gather.8
  73.3 68.5 all-gather.10
  143.3 31.6 all-gather.12
  176.4 64.8 all-gather.16
  242.7 64.8 all-gather.14
  309.1 64.8 all-gather.18
  813.9 173.3 all-reduce.6
  992.4 101.7 all-reduce.4
